TPU v7x, 32 devices: a whole 2x2x4 slice. The times are simulated.
32 devices in a mesh: dp: 4 (over z), row: 2 (over x), col: 4 (over y, core).
Axes of the slice: x: 2, y: 2, z: 4, core: 2. Of those that a mesh axis runs over, the one named last changes fastest.
Arguments:
- tokens: bfloat16 [8192, 1024], P(('dp', 'row'), 'col'), may hold values from -6 to 6
- lengths: int32 [4, 9], P('dp'), may hold values from 1 to 512, as said below
- ln1_gain: bfloat16 [1024], P('col'), may hold values from 0.5 to 1.5
- ln1_bias: bfloat16 [1024], P('col'), may hold values from -3 to 3
- qkv_weight: bfloat16 [1024, 3, 1024], P('col', None, 'row'), may hold values from -0.1875 to 0.1875
- qv_bias: bfloat16 [2, 1024], P(None, ('row', 'col')), may hold values from -3 to 3
- out_weight: bfloat16 [1024, 1024], P('row', 'col'), may hold values from -0.5 to 0.5
- out_bias: bfloat16 [1024], P('col'), may hold values from -3 to 3
- ln2_gain: bfloat16 [1024], P('col'), may hold values from 0.5 to 1.5
- ln2_bias: bfloat16 [1024], P('col'), may hold values from -3 to 3
- up_weight: bfloat16 [1024, 4096], P('col', 'row'), may hold values from -0.1875 to 0.1875
- up_bias: bfloat16 [4096], P(('row', 'col')), may hold values from -3 to 3
- down_weight: bfloat16 [4096, 1024], P('row', 'col'), may hold values from -0.09375 to 0.09375
- down_bias: bfloat16 [1024], P('col'), may hold values from -3 to 3
- cotangent: bfloat16 [8192, 1024], P(('dp', 'row'), 'col'), may hold values from -6 to 6
Outputs:
- block_out: bfloat16 [8192, 1024], P(('dp', 'row'), 'col')
- grad_tokens: float32 [8192, 1024], P(('dp', 'row'), 'col')
- grad_ln1_gain: float32 [1024], P('col')
- grad_ln1_bias: float32 [1024], P('col')
- grad_qkv_weight: float32 [1024, 3, 1024], P('col', None, 'row')
- grad_qv_bias: float32 [2, 1024], P(None, ('row', 'col'))
- grad_out_weight: float32 [1024, 1024], P('row', 'col')
- grad_out_bias: float32 [1024], P('col')
- grad_ln2_gain: float32 [1024], P('col')
- grad_ln2_bias: float32 [1024], P('col')
- grad_up_weight: float32 [1024, 4096], P('col', 'row')
- grad_up_bias: float32 [4096], P(('row', 'col'))
- grad_down_weight: float32 [4096, 1024], P('row', 'col')
- grad_down_bias: float32 [1024], P('col')
Inputs may be any that keep to these rules, and one draw needn't show every extreme that they name: Row g holds the lengths of the 9 sequences packed in order into the 2048 tokens of dp group g; they sum to 2048, and the longest of each row is exactly 512.
All inputs are finite; a program needn't handle non-finite values.
Results may differ from a plain program's by a relative error of at most 0.014.
Values may be sent and summed in bfloat16 or wider, within the bound.
A program may use at most 192 MiB of HBM per device.

v0:
```python
import math

import jax
import jax.numpy as jnp
from jax import lax
from jax.sharding import PartitionSpec as P

HD = 64
HEADS = 16


epsilon = 1e-05
masked = -1e30


def gelu_tanh(values):
    return jax.nn.gelu(values, approximate=True)


def feature_sums(first, second):
    return lax.psum((jnp.sum(first, axis=-1), jnp.sum(second, axis=-1)), "col")


def norm_forward(values, gain, shift):
    width = values.shape[-1] * lax.axis_size("col")
    total, squares = feature_sums(values, values * values)
    mean = total / width
    inverse = lax.rsqrt(squares / width - mean * mean + epsilon)
    centred = (values - mean[:, None]) * inverse[:, None]
    normed = centred * gain.astype(jnp.float32) + shift.astype(jnp.float32)
    return (normed.astype(jnp.bfloat16), centred, inverse)


def norm_backward(upstream, centred, inverse, gain):
    width = upstream.shape[-1] * lax.axis_size("col")
    scaled = upstream * gain.astype(jnp.float32)
    total, mixed = feature_sums(scaled, scaled * centred)
    back = inverse[:, None] * (scaled - total[:, None] / width - centred * mixed[:, None] / width)
    return (back, jnp.sum(upstream * centred, axis=0), jnp.sum(upstream, axis=0))


def contract(left, matrix, flip):
    if flip:
        return lax.dot_general(
            left, matrix, (((1,), (1,)), ((), ())), preferred_element_type=jnp.float32
        )
    return jnp.dot(left, matrix, preferred_element_type=jnp.float32)


def outer_sum(left, right):
    return lax.dot_general(
        left, right, (((0,), (0,)), ((), ())), preferred_element_type=jnp.float32
    )


def rows_then_cols(shard, matrix, flip, groups):
    rows = lax.all_gather(shard, "row", axis=0, tiled=True)
    partial_sum = contract(rows, matrix, flip)
    shaped = partial_sum.reshape(rows.shape[0], groups, -1)
    return (rows, lax.psum_scatter(shaped, "col", scatter_dimension=2, tiled=True))


def cols_then_rows(shard, matrix, flip):
    columns = lax.all_gather(shard, "col", axis=2, tiled=True)
    flat = columns.reshape(columns.shape[0], -1)
    partial_sum = contract(flat, matrix, flip)
    return (flat, lax.psum_scatter(partial_sum, "row", scatter_dimension=0, tiled=True))


def feed_partial(shard, matrix, flip):
    rows = lax.all_gather(shard, "row", axis=0, tiled=True)
    partial_sum = contract(rows, matrix, flip)
    shaped = partial_sum.reshape(rows.shape[0], 1, -1)
    summed = lax.psum_scatter(shaped, "col", scatter_dimension=2, tiled=True)
    return (rows, summed.reshape(rows.shape[0], -1))


def block_scores(query, keys, rows_at, keys_at, rows_seq, keys_seq, slopes, scale):
    scores = jnp.einsum("qhd,khd->hqk", query, keys, preferred_element_type=jnp.float32) * scale
    distance = (keys_at[None, :] - rows_at[:, None]).astype(jnp.float32)
    scores = scores + slopes[:, None, None] * distance[None]
    allowed = (rows_seq[:, None] == keys_seq[None, :]) & (keys_at[None, :] <= rows_at[:, None])
    return jnp.where(allowed[None], scores, masked)


def attend(query, keys, values, sequence, slopes, scale):
    count = query.shape[0]
    places = jnp.arange(count, dtype=jnp.int32)
    block = min(512, count)
    outputs = []
    totals = []
    for index in range(count // block):
        start = index * block
        stop = start + block
        scores = block_scores(
            query[start:stop],
            keys[:stop],
            places[start:stop],
            places[:stop],
            sequence[start:stop],
            sequence[:stop],
            slopes,
            scale,
        )
        peak = jnp.max(scores, axis=-1, keepdims=True)
        spread = jnp.exp(scores - peak)
        total = jnp.sum(spread, axis=-1, keepdims=True)
        weights = (spread / total).astype(jnp.bfloat16)
        outputs.append(
            jnp.einsum("hqk,khd->qhd", weights, values[:stop], preferred_element_type=jnp.float32)
        )
        totals.append(peak + jnp.log(total))
    return (jnp.concatenate(outputs, axis=0), totals)


def attend_back(query, keys, values, sequence, slopes, scale, totals, upstream):
    count = query.shape[0]
    places = jnp.arange(count, dtype=jnp.int32)
    block = min(512, count)
    grad_query = []
    grad_keys = jnp.zeros(keys.shape, jnp.float32)
    grad_values = jnp.zeros(values.shape, jnp.float32)
    for index in range(count // block):
        start = index * block
        stop = start + block
        scores = block_scores(
            query[start:stop],
            keys[:stop],
            places[start:stop],
            places[:stop],
            sequence[start:stop],
            sequence[:stop],
            slopes,
            scale,
        )
        probability = jnp.exp(scores - totals[index])
        rounded = probability.astype(jnp.bfloat16)
        above = upstream[start:stop]
        grad_prob = jnp.einsum(
            "qhd,khd->hqk", above, values[:stop], preferred_element_type=jnp.float32
        )
        centre = jnp.sum(probability * grad_prob, axis=-1, keepdims=True)
        grad_scores = (probability * (grad_prob - centre)).astype(jnp.bfloat16)
        grad_query.append(
            jnp.einsum("hqk,khd->qhd", grad_scores, keys[:stop], preferred_element_type=jnp.float32)
            * scale
        )
        grad_keys = grad_keys.at[:stop].add(
            jnp.einsum(
                "hqk,qhd->khd", grad_scores, query[start:stop], preferred_element_type=jnp.float32
            )
            * scale
        )
        grad_values = grad_values.at[:stop].add(
            jnp.einsum("hqk,qhd->khd", rounded, above, preferred_element_type=jnp.float32)
        )
    return (jnp.concatenate(grad_query, axis=0), grad_keys, grad_values)


def on_device(
    tokens,
    lengths,
    ln1_gain,
    ln1_bias,
    qkv_weight,
    qv_bias,
    out_weight,
    out_bias,
    ln2_gain,
    ln2_bias,
    up_weight,
    up_bias,
    down_weight,
    down_bias,
    cotangent,
):
    count = tokens.shape[0] * lax.axis_size("row")
    head_size = HD
    local_heads = qkv_weight.shape[2] // lax.axis_size("col") // head_size
    first_head = (
        lax.axis_index("row") * lax.axis_size("col") + lax.axis_index("col")
    ) * local_heads
    slopes = jnp.exp2(
        -8.0
        * (first_head + jnp.arange(local_heads, dtype=jnp.int32) + 1).astype(jnp.float32)
        / HEADS
    )
    scale = 1.0 / math.sqrt(head_size)
    ends = jnp.cumsum(lengths[0])
    places = jnp.arange(count, dtype=jnp.int32)
    sequence = jnp.sum((places[:, None] >= ends[None, :]).astype(jnp.int32), axis=1)
    residual = tokens.astype(jnp.float32)
    normed_one, centred_one, inverse_one = norm_forward(residual, ln1_gain, ln1_bias)
    merged_flat = qkv_weight.reshape(qkv_weight.shape[0], -1)
    normed_rows, projected = rows_then_cols(normed_one, merged_flat, False, 3)
    bias_three = jnp.stack([qv_bias[0], jnp.zeros_like(qv_bias[0]), qv_bias[1]]).astype(jnp.float32)
    projected = (projected + bias_three[None]).astype(jnp.bfloat16)
    query = projected[:, 0].reshape(count, local_heads, head_size)
    keys = projected[:, 1].reshape(count, local_heads, head_size)
    values = projected[:, 2].reshape(count, local_heads, head_size)
    context, totals = attend(query, keys, values, sequence, slopes, scale)
    context = context.reshape(count, -1).astype(jnp.bfloat16)
    context_columns, attention_out = cols_then_rows(
        context.reshape(count, 1, -1), out_weight, False
    )
    middle = residual + attention_out + out_bias.astype(jnp.float32)
    normed_two, centred_two, inverse_two = norm_forward(middle, ln2_gain, ln2_bias)
    normed_two_rows, hidden = feed_partial(normed_two, up_weight, False)
    hidden = hidden + up_bias.astype(jnp.float32)
    activated, gelu_pull = jax.vjp(gelu_tanh, hidden)
    activated = activated.astype(jnp.bfloat16)
    active_columns, feed_out = cols_then_rows(activated.reshape(count, 1, -1), down_weight, False)
    block_out = (middle + feed_out + down_bias.astype(jnp.float32)).astype(jnp.bfloat16)
    upstream = cotangent.astype(jnp.float32)
    cotangent_rows, grad_active = feed_partial(cotangent, down_weight, True)
    grad_hidden = gelu_pull(grad_active)[0].astype(jnp.bfloat16)
    grad_up_bias = jnp.sum(grad_hidden.astype(jnp.float32), axis=0)
    hidden_columns, grad_normed_two = cols_then_rows(
        grad_hidden.reshape(count, 1, -1), up_weight, True
    )
    grad_up_weight = outer_sum(normed_two_rows, hidden_columns)
    grad_down_weight = outer_sum(active_columns, cotangent_rows)
    grad_down_bias = jnp.sum(upstream, axis=0)
    back_two, grad_ln2_gain, grad_ln2_bias = norm_backward(
        grad_normed_two, centred_two, inverse_two, ln2_gain
    )
    grad_middle = upstream + back_two
    grad_attention = grad_middle.astype(jnp.bfloat16)
    grad_out_bias = jnp.sum(grad_middle, axis=0)
    attention_rows, grad_context = rows_then_cols(grad_attention, out_weight, True, 1)
    grad_out_weight = outer_sum(context_columns, attention_rows)
    grad_context = grad_context.reshape(count, local_heads, head_size).astype(jnp.bfloat16)
    grad_query, grad_keys, grad_values = attend_back(
        query, keys, values, sequence, slopes, scale, totals, grad_context
    )
    grad_projected = jnp.stack(
        [
            grad_query.reshape(count, -1),
            grad_keys.reshape(count, -1),
            grad_values.reshape(count, -1),
        ],
        axis=1,
    ).astype(jnp.bfloat16)
    summed_rows = jnp.sum(grad_projected.astype(jnp.float32), axis=0)
    grad_qv_bias = jnp.stack([summed_rows[0], summed_rows[2]])
    projected_columns, grad_normed_one = cols_then_rows(grad_projected, merged_flat, True)
    grad_qkv_weight = outer_sum(normed_rows, projected_columns).reshape(qkv_weight.shape)
    back_one, grad_ln1_gain, grad_ln1_bias = norm_backward(
        grad_normed_one, centred_one, inverse_one, ln1_gain
    )
    grad_tokens = grad_middle + back_one
    weight_sums = (
        lax.psum(grad_qkv_weight.astype(jnp.bfloat16), "dp").astype(jnp.float32),
        lax.psum(grad_qv_bias.astype(jnp.bfloat16), "dp").astype(jnp.float32),
        lax.psum(grad_out_weight.astype(jnp.bfloat16), "dp").astype(jnp.float32),
        lax.psum(grad_up_weight.astype(jnp.bfloat16), "dp").astype(jnp.float32),
        lax.psum(grad_up_bias.astype(jnp.bfloat16), "dp").astype(jnp.float32),
        lax.psum(grad_down_weight.astype(jnp.bfloat16), "dp").astype(jnp.float32),
    )
    vector_sums = lax.psum(
        (grad_ln1_gain, grad_ln1_bias, grad_out_bias, grad_ln2_gain, grad_ln2_bias, grad_down_bias),
        ("dp", "row"),
    )
    return (
        block_out,
        grad_tokens,
        vector_sums[0],
        vector_sums[1],
        weight_sums[0],
        weight_sums[1],
        weight_sums[2],
        vector_sums[2],
        vector_sums[3],
        vector_sums[4],
        weight_sums[3],
        weight_sums[4],
        weight_sums[5],
        vector_sums[5],
    )


def solution(mesh):
    return jax.shard_map(
        on_device,
        mesh=mesh,
        in_specs=(
            P(("dp", "row"), "col"),
            P("dp", None),
            P("col"),
            P("col"),
            P("col", None, "row"),
            P(None, ("row", "col")),
            P("row", "col"),
            P("col"),
            P("col"),
            P("col"),
            P("col", "row"),
            P(("row", "col")),
            P("row", "col"),
            P("col"),
            P(("dp", "row"), "col"),
        ),
        out_specs=(
            P(("dp", "row"), "col"),
            P(("dp", "row"), "col"),
            P("col"),
            P("col"),
            P("col", None, "row"),
            P(None, ("row", "col")),
            P("row", "col"),
            P("col"),
            P("col"),
            P("col"),
            P("col", "row"),
            P(("row", "col")),
            P("row", "col"),
            P("col"),
        ),
        check_vma=False,
    )
```

profile of v0, /device:TPU:0, one launch (start us, length us, event | category | flops | bytes accessed | tf_op | source)
XLA Modules:
  0.0 1136.3 jit_solution(8594831667203293355)
XLA Ops:
  10.0 8.5 all-reduce.6
  22.8 20.3 %all-gather.9.cloned.1.call-done = bf16[2048,256]{1,0:T(8,128)(2,1)} async-done(((bf16[1024,256]{1,0:T(8,128)(2,1)}), bf16[2048,256]{1,0:T(8,128)(2,1)}) %all-gather.9.cloned.1.call-update) | async-done | bytes 1048592 | tf_op jit(solution)/shard_map/all_gather | solution.py:57
  65.6 84.3 %reduce-scatter.9.cloned.1.call-done = f32[2048,3,128]{2,0,1:T(8,128)} async-done(((f32[2048,3,512]{2,0,1:T(8,128)}), f32[2048,3,128]{2,0,1:T(8,128)}) %reduce-scatter.9.cloned.1.call-update) | async-done | bytes 3145744 | tf_op jit(solution)/shard_map/reduce_scatter | solution.py:60
  192.7 22.7 %all-gather.11.cloned.1.call-done = bf16[2048,1,512]{0,2,1:T(8,128)(2,1)} async-done(((bf16[2048,1,128]{0,2,1:T(8,128)(2,1)}), bf16[2048,1,512]{0,2,1:T(8,128)(2,1)}) %all-gather.11.cloned.1.call-update) | async-done | bytes 2097168 | tf_op jit(solution)/shard_map/all_gather | solution.py:64
  221.6 29.5 %reduce-scatter.11.cloned.1.call-done = f32[1024,256]{1,0:T(8,128)} async-done(((f32[2048,256]{1,0:T(8,128)}), f32[1024,256]{1,0:T(8,128)}) %reduce-scatter.11.cloned.1.call-update) | async-done | bytes 1048592 | tf_op jit(solution)/shard_map/reduce_scatter | solution.py:67
  264.3 9.6 all-gather.17.cloned.1.call-done
  273.9 10.0 convolution_bitcast_fusion
  284.4 12.9 %all-gather.13.cloned.1.call-done = bf16[2048,256]{1,0:T(8,128)(2,1)} async-done(((bf16[1024,256]{1,0:T(8,128)(2,1)}), bf16[2048,256]{1,0:T(8,128)(2,1)}) %all-gather.13.cloned.1.call-update) | async-done | bytes 1048592 | tf_op jit(solution)/shard_map/all_gather | solution.py:71
  297.3 9.9 convolution_bitcast_fusion.1
  308.0 118.2 %reduce-scatter.17.cloned.1.call-done = f32[2048,1,512]{2,0,1:T(8,128)} async-done(((f32[2048,1,2048]{2,0,1:T(8,128)}), f32[2048,1,512]{2,0,1:T(8,128)}) %reduce-scatter.17.cloned.1.call-update) | async-done | bytes 4194320 | tf_op jit(solution)/shard_map/reduce_scatter | solution.py:74
  426.2 128.7 %reduce-scatter.13.cloned.1.call-done = f32[2048,1,512]{2,0,1:T(8,128)} async-done(((f32[2048,1,2048]{2,0,1:T(8,128)}), f32[2048,1,512]{2,0,1:T(8,128)}) %reduce-scatter.13.cloned.1.call-update) | async-done | bytes 4194320 | tf_op jit(solution)/shard_map/reduce_scatter | solution.py:74
  562.3 57.8 %all-gather.19.cloned.1.call-done = bf16[2048,1,2048]{2,0,1:T(8,128)(2,1)} async-done(((bf16[2048,1,512]{2,0,1:T(8,128)(2,1)}), bf16[2048,1,2048]{2,0,1:T(8,128)(2,1)}) %all-gather.19.cloned.1.call-update) | async-done | bytes 8388624 | tf_op jit(solution)/shard_map/all_gather | solution.py:64
  627.3 53.2 %all-gather.15.cloned.1.call-done = bf16[2048,1,2048]{2,0,1:T(8,128)(2,1)} async-done(((bf16[2048,1,512]{2,0,1:T(8,128)(2,1)}), bf16[2048,1,2048]{2,0,1:T(8,128)(2,1)}) %all-gather.15.cloned.1.call-update) | async-done | bytes 8388624 | tf_op jit(solution)/shard_map/all_gather | solution.py:64
  688.5 26.8 %reduce-scatter.19.cloned.1.call-done = f32[1024,256]{1,0:T(8,128)} async-done(((f32[2048,256]{1,0:T(8,128)}), f32[1024,256]{1,0:T(8,128)}) %reduce-scatter.19.cloned.1.call-update) | async-done | bytes 1048592 | tf_op jit(solution)/shard_map/reduce_scatter | solution.py:67
  726.2 23.7 %reduce-scatter.15.cloned.1.call-done = f32[1024,256]{1,0:T(8,128)} async-done(((f32[2048,256]{1,0:T(8,128)}), f32[1024,256]{1,0:T(8,128)}) %reduce-scatter.15.cloned.1.call-update) | async-done | bytes 1048592 | tf_op jit(solution)/shard_map/reduce_scatter | solution.py:67
  755.4 21.3 %all-gather.21.cloned.1.call-done = bf16[2048,256]{1,0:T(8,128)(2,1)} async-done(((bf16[1024,256]{1,0:T(8,128)(2,1)}), bf16[2048,256]{1,0:T(8,128)(2,1)}) %all-gather.21.cloned.1.call-update) | async-done | bytes 1048592 | tf_op jit(solution)/shard_map/all_gather | solution.py:57
  781.1 44.3 %reduce-scatter.21.cloned.1.call-done = f32[2048,1,128]{2,0,1:T(8,128)} async-done(((f32[2048,1,512]{2,0,1:T(8,128)}), f32[2048,1,128]{2,0,1:T(8,128)}) %reduce-scatter.21.cloned.1.call-update) | async-done | bytes 1048592 | tf_op jit(solution)/shard_map/reduce_scatter | solution.py:60
  886.4 8.1 fusion.42
  895.9 30.8 %all-gather.23.cloned.1.call-done = bf16[2048,3,512]{2,0,1:T(8,128)(2,1)} async-done(((bf16[2048,3,128]{2,0,1:T(8,128)(2,1)}), bf16[2048,3,512]{2,0,1:T(8,128)(2,1)}) %all-gather.23.cloned.1.call-update) | async-done | bytes 6291472 | tf_op jit(solution)/shard_map/all_gather | solution.py:64
  926.7 8.9 copy.119
  952.7 12.2 %all-reduce.7 = (bf16[2,128]{1,0:T(2,128)(2,1)S(1)}, bf16[512]{0:T(512)(128)(2,1)S(1)}) all-reduce(bf16[2,128]{1,0:T(2,128)(2,1)S(1)} %pad_maximum_fusion.3, bf16[512]{0:T(512)(128)(2,1)S(1)} %fusion.80), channel_id=1, replica_groups=mesh['dp'=4,'row'=2,'col'=4] {'dp'}, use_global_device_ids=true, to_apply=%region_44.45 | all-reduce | flops 768 | bytes 3072 | tf_op jit(solution)/shard_map/psum | solution.py:254
  966.0 97.7 %all-reduce.11.cloned.1.call-done = (bf16[256,3,512]{2,0,1:T(8,128)(2,1)}, bf16[512,256]{1,0:T(8,128)(2,1)}, bf16[256,2048]{1,0:T(8,128)(2,1)}, bf16[2048,256]{1,0:T(8,128)(2,1)}) async-done(((bf16[256,3,512]{2,0,1:T(8,128)(2,1)}, bf16[512,256]{1,0:T(8,128)(2,1)}, bf16[256,2048]{1,0:T(8,128)(2,1)}, bf16[2048,256]{1,0:T(8,128)(2,1)}), (bf16[256,3,512]{2,0,1:T(8,128)(2,1)}, bf16[512,256]{1,0:T(8,128)(2,1)}, ...) | async-done | bytes 3145744 | tf_op jit(solution)/shard_map/psum | solution.py:253
  1072.5 24.1 %reduce-scatter.23.cloned.1.call-done = f32[1024,256]{1,0:T(8,128)} async-done(((f32[2048,256]{1,0:T(8,128)}), f32[1024,256]{1,0:T(8,128)}) %reduce-scatter.23.cloned.1.call-update) | async-done | bytes 1048592 | tf_op jit(solution)/shard_map/reduce_scatter | solution.py:67
  1105.6 21.3 %all-reduce.2 = (f32[256]{0:T(256)}, f32[256]{0:T(256)}, f32[256]{0:T(256)}, f32[256]{0:T(256)}, f32[256]{0:T(256)}, /*index=5*/f32[256]{0:T(256)}) all-reduce(f32[256]{0:T(256)S(1)} %get-tuple-element.128, f32[256]{0:T(256)S(1)} %get-tuple-element.133, f32[256]{0:T(256)S(1)} %copy-done.71, ...), channel_id=1, replica_groups=mesh['dp'=4,'row'=2,'col'=4] {'dp','row'}, use_global_device_ids=true, to_apply=%region_39.40 | all-reduce | flops 1536 | bytes 12288 | tf_op jit(solution)/shard_map/psum | solution.py:260
  (351 shorter events, 236.0 us)
Async XLA Ops:
  7.2 290.1 %copy-start = (bf16[256,2048]{1,0:T(8,128)(2,1)S(1)}, bf16[256,2048]{1,0:T(8,128)(2,1)}, u32[]{:S(2)}) copy-start(bf16[256,2048]{1,0:T(8,128)(2,1)} %param.45) | copy-start | bytes 3145732
  7.2 35.9 %all-gather.9.cloned.1.call-start = ((), (), s32[]{:S(2)}) async-start(), calls=%async_computation.8 | async-start | bytes 1572864 | tf_op jit(solution)/shard_map/all_gather | solution.py:57
  21.4 128.5 %reduce-scatter.9.cloned.1.call-start = ((), (), s32[]{:S(2)}) async-start(), calls=%async_computation.9 | async-start | bytes 15728640 | tf_op jit(solution)/shard_map/reduce_scatter | solution.py:60
  50.7 164.7 %all-gather.11.cloned.1.call-start = ((), (), s32[]{:S(2)}) async-start(), calls=%async_computation.10 | async-start | bytes 2621440 | tf_op jit(solution)/shard_map/all_gather | solution.py:64
  192.7 58.4 %reduce-scatter.11.cloned.1.call-start = ((), (), s32[]{:S(2)}) async-start(), calls=%async_computation.11 | async-start | bytes 3145728 | tf_op jit(solution)/shard_map/reduce_scatter | solution.py:67
  219.1 54.8 %all-gather.17.cloned.1.call-start = ((), (), s32[]{:S(2)}) async-start(), calls=%async_computation.16 | async-start | bytes 1572864 | tf_op jit(solution)/shard_map/all_gather | solution.py:71
  219.7 77.6 %all-gather.13.cloned.1.call-start = ((), (), s32[]{:S(2)}) async-start(), calls=%async_computation.12 | async-start | bytes 1572864 | tf_op jit(solution)/shard_map/all_gather | solution.py:71
  219.8 64.1 %copy-start.66 = (f32[256]{0:T(256)}, f32[256]{0:T(256)S(1)}, u32[]{:S(2)}) copy-start(f32[256]{0:T(256)S(1)} %convert_element_type.209) | copy-start | bytes 3076
  264.3 162.0 %reduce-scatter.17.cloned.1.call-start = ((), (), s32[]{:S(2)}) async-start(), calls=%async_computation.17 | async-start | bytes 20971520 | tf_op jit(solution)/shard_map/reduce_scatter | solution.py:74
  283.9 271.1 %reduce-scatter.13.cloned.1.call-start = ((), (), s32[]{:S(2)}) async-start(), calls=%async_computation.13 | async-start | bytes 20971520 | tf_op jit(solution)/shard_map/reduce_scatter | solution.py:74
  307.3 312.9 %all-gather.19.cloned.1.call-start = ((), (), s32[]{:S(2)}) async-start(), calls=%async_computation.18 | async-start | bytes 10485760 | tf_op jit(solution)/shard_map/all_gather | solution.py:64
  308.0 253.6 %copy-start.55 = (f32[512]{0:T(512)}, f32[512]{0:T(512)S(1)}, u32[]{:S(2)}) copy-start(f32[512]{0:T(512)S(1)} %convert_element_type.212) | copy-start | bytes 6148
  561.7 118.8 %all-gather.15.cloned.1.call-start = ((), (), s32[]{:S(2)}) async-start(), calls=%async_computation.14 | async-start | bytes 10485760 | tf_op jit(solution)/shard_map/all_gather | solution.py:64
  562.3 153.0 %reduce-scatter.19.cloned.1.call-start = ((), (), s32[]{:S(2)}) async-start(), calls=%async_computation.19 | async-start | bytes 3145728 | tf_op jit(solution)/shard_map/reduce_scatter | solution.py:67
  627.3 60.6 %copy-start.77 = (bf16[256]{0:T(256)(128)(2,1)S(1)}, bf16[256]{0:T(256)(128)(2,1)}, u32[]{:S(2)}) copy-start(bf16[256]{0:T(256)(128)(2,1)} %param.48) | copy-start | bytes 1540
  627.3 88.0 %copy-start.7 = (f32[1024,256]{1,0:T(8,128)S(1)}, f32[1024,256]{1,0:T(8,128)}, u32[]{:S(2)}) copy-start(f32[1024,256]{1,0:T(8,128)} %get-tuple-element.162) | copy-start | bytes 3145732
  627.3 122.6 %reduce-scatter.15.cloned.1.call-start = ((), (), s32[]{:S(2)}) async-start(), calls=%async_computation.15 | async-start | bytes 3145728 | tf_op jit(solution)/shard_map/reduce_scatter | solution.py:67
  687.8 88.9 %all-gather.21.cloned.1.call-start = ((), (), s32[]{:S(2)}) async-start(), calls=%async_computation.20 | async-start | bytes 1572864 | tf_op jit(solution)/shard_map/all_gather | solution.py:57
  755.3 70.0 %reduce-scatter.21.cloned.1.call-start = ((), (), s32[]{:S(2)}) async-start(), calls=%async_computation.21 | async-start | bytes 5242880 | tf_op jit(solution)/shard_map/reduce_scatter | solution.py:60
  780.7 146.0 %all-gather.23.cloned.1.call-start = ((), (), s32[]{:S(2)}) async-start(), calls=%async_computation.22 | async-start | bytes 7864320 | tf_op jit(solution)/shard_map/all_gather | solution.py:64
  879.3 184.4 %all-reduce.11.cloned.1.call-start = ((), (), s32[]{:S(2)}) async-start(), calls=%async_computation.24 | async-start | bytes 6291456 | tf_op jit(solution)/shard_map/psum | solution.py:253
  941.2 155.4 %reduce-scatter.23.cloned.1.call-start = ((), (), s32[]{:S(2)}) async-start(), calls=%async_computation.23 | async-start | bytes 3145728 | tf_op jit(solution)/shard_map/reduce_scatter | solution.py:67
  1068.1 58.7 %copy-start.11 = (f32[1024,256]{1,0:T(8,128)S(1)}, f32[1024,256]{1,0:T(8,128)}, u32[]{:S(2)}) copy-start(f32[1024,256]{1,0:T(8,128)} %copy-done.10) | copy-start | bytes 3145732
  1071.0 58.5 %copy-start.1 = (bf16[256,2048]{1,0:T(8,128)(2,1)S(1)}, bf16[256,2048]{1,0:T(8,128)(2,1)}, u32[]{:S(2)}) copy-start(bf16[256,2048]{1,0:T(8,128)(2,1)} %param.45) | copy-start | bytes 3145732
  (83 other events, 853.8 us)
Sparse Core Ops, SparseCore 0:
  21.5 21.5 all-gather.8
  50.9 99.0 reduce-scatter.8
  192.8 22.6 all-gather.10
  219.2 31.8 reduce-scatter.10
  252.6 21.3 all-gather.16
  276.0 21.2 all-gather.12
  300.0 126.1 reduce-scatter.16
  428.8 126.1 reduce-scatter.12
  561.8 58.2 all-gather.18
  622.2 58.2 all-gather.14
  683.4 31.8 reduce-scatter.18
  718.0 31.8 reduce-scatter.14
  755.4 21.2 all-gather.20
  780.9 44.4 reduce-scatter.20
  879.5 47.2 all-gather.22
  941.3 122.3 all-reduce.10
  1065.8 30.7 reduce-scatter.22
where the time goes:
time: 1140 us
  waiting for transfers between devices  807 us (71%)
  matrix products  123 us (11%)
  other arithmetic  79.7 us (7%)
  blocking collectives  64.3 us (6%)
  local copies, waits for them, and re-layouts  44.6 us (4%)
  between operations  15.5 us (1%)
    reduce_scatter x2, waiting for transfers between devices, feed_partial(): summed = lax.psum_scatter(shaped, 'col', scatter_dimension=2, tiled=True)  247 us
    all_gather x4, waiting for transfers between devices, cols_then_rows(): columns = lax.all_gather(shard, 'col', axis=2, tiled=True)  165 us
    reduce_scatter x2, waiting for transfers between devices, rows_then_cols(): lax.psum_scatter(shaped, 'col', scatter_dimension=2, tiled=True)  129 us
    reduce_scatter x4, waiting for transfers between devices, cols_then_rows(): lax.psum_scatter(partial_sum, 'row', scatter_dimension=0, tiled=True)  104 us
    psum x1, waiting for transfers between devices, on_device(): lax.psum(grad_qkv_weight.astype(jnp.bfloat16), 'dp').astype(jnp.float32)  97.7 us
    all_gather x2, waiting for transfers between devices, rows_then_cols(): rows = lax.all_gather(shard, 'row', axis=0, tiled=True)  41.6 us
    psum x4, blocking collectives, feature_sums(): return lax.psum((jnp.sum(first, axis=-1), jnp.sum(second, axis=-1)), 'col')  30.9 us
    dot_general x4, matrix products, contract(): return jnp.dot(left, matrix, preferred_element_type=jnp.float32)  28.4 us
  transfers between devices with their start and end apart: 17, of which 17 were waited for; matrix products, arithmetic and copies ran while one was open for 9% of the time, Pallas kernels for 0%

commit v1 on v0

v1 whole, which is shorter than its diff:
```python
import functools
import math

import jax
import jax.numpy as jnp
from jax import lax
from jax.experimental import pallas as pl
from jax.experimental.pallas import tpu as pltpu
from jax.sharding import PartitionSpec as P

HD = 64
HEADS = 16
LONGEST = 512
BLOCK = 256

epsilon = 1e-05
masked = -1e30
GROUP = ("row", "col")
VMEM_LIMIT = 48 * 1024 * 1024


def gelu_tanh(values):
    return jax.nn.gelu(values, approximate=True)


def norm_stats(values):
    mean = jnp.mean(values, axis=-1, keepdims=True)
    away = values - mean
    inverse = lax.rsqrt(jnp.mean(away * away, axis=-1, keepdims=True) + epsilon)
    return away * inverse, inverse


def norm_apply(centred, gain, shift):
    normed = centred * gain.astype(jnp.float32) + shift.astype(jnp.float32)
    return normed.astype(jnp.bfloat16)


def norm_backward(upstream, centred, inverse, gain):
    scaled = upstream * gain.astype(jnp.float32)
    total = jnp.mean(scaled, axis=-1, keepdims=True)
    mixed = jnp.mean(scaled * centred, axis=-1, keepdims=True)
    back = inverse * (scaled - total - centred * mixed)
    return (back, jnp.sum(upstream * centred, axis=0), jnp.sum(upstream, axis=0))


def product(left, right):
    return jnp.dot(left, right, preferred_element_type=jnp.float32)


def product_flip(left, right):
    return lax.dot_general(left, right, (((1,), (1,)), ((), ())), preferred_element_type=jnp.float32)


def outer_sum(left, right):
    return lax.dot_general(left, right, (((0,), (0,)), ((), ())), preferred_element_type=jnp.float32)


def head_parts(q_ref, k_ref, v_ref, first, slope, head, start, begin, window, scale):
    lanes = slice(head * HD, (head + 1) * HD)
    query = q_ref[pl.ds(start, BLOCK), lanes]
    keys = k_ref[pl.ds(begin, window), lanes]
    values = v_ref[pl.ds(begin, window), lanes]
    scores = product_flip(query, keys) * scale
    rows_at = start + lax.broadcasted_iota(jnp.int32, (BLOCK, window), 0)
    keys_at = begin + lax.broadcasted_iota(jnp.int32, (BLOCK, window), 1)
    distance = keys_at - rows_at
    scores = scores + slope * distance.astype(jnp.float32)
    scores = jnp.where((distance <= 0) & (keys_at >= first), scores, masked)
    peak = jnp.max(scores, axis=-1, keepdims=True)
    spread = jnp.exp(scores - peak)
    total = jnp.sum(spread, axis=-1, keepdims=True)
    return query, keys, values, spread * (1.0 / total)


def attend_kernel(heads, window, scale, slopes_ref, first_ref, q_ref, k_ref, v_ref, out_ref):
    start = pl.multiple_of(pl.program_id(0) * BLOCK, BLOCK)
    begin = pl.multiple_of(jnp.maximum(start + BLOCK - window, 0), BLOCK)
    first = first_ref[pl.ds(start, BLOCK), :]
    parts = []
    for head in range(heads):
        _, _, values, probability = head_parts(
            q_ref, k_ref, v_ref, first, slopes_ref[head], head, start, begin, window, scale
        )
        parts.append(product(probability.astype(jnp.bfloat16), values))
    out_ref[pl.ds(start, BLOCK), :] = jnp.concatenate(parts, axis=1).astype(jnp.bfloat16)


def attend_back_kernel(
    heads, window, scale, slopes_ref, first_ref, q_ref, k_ref, v_ref, up_ref, out_ref, dk_ref, dv_ref
):
    step = pl.program_id(0)

    @pl.when(step == 0)
    def _():
        dk_ref[...] = jnp.zeros_like(dk_ref)
        dv_ref[...] = jnp.zeros_like(dv_ref)

    start = pl.multiple_of(step * BLOCK, BLOCK)
    begin = pl.multiple_of(jnp.maximum(start + BLOCK - window, 0), BLOCK)
    first = first_ref[pl.ds(start, BLOCK), :]
    grads = []
    key_grads = []
    value_grads = []
    for head in range(heads):
        query, keys, values, probability = head_parts(
            q_ref, k_ref, v_ref, first, slopes_ref[head], head, start, begin, window, scale
        )
        above = up_ref[pl.ds(start, BLOCK), head * HD : (head + 1) * HD]
        grad_prob = product_flip(above, values)
        centre = jnp.sum(probability * grad_prob, axis=-1, keepdims=True)
        grad_scores = (probability * (grad_prob - centre)).astype(jnp.bfloat16)
        grads.append(product(grad_scores, keys) * scale)
        key_grads.append(outer_sum(grad_scores, query) * scale)
        value_grads.append(outer_sum(probability.astype(jnp.bfloat16), above))
    width = heads * HD
    out_ref[pl.ds(start, BLOCK), 0:width] = jnp.concatenate(grads, axis=1).astype(jnp.bfloat16)
    dk_ref[pl.ds(begin, window), :] += jnp.concatenate(key_grads, axis=1)
    dv_ref[pl.ds(begin, window), :] += jnp.concatenate(value_grads, axis=1)

    @pl.when(step == pl.num_programs(0) - 1)
    def _():
        out_ref[:, width : 2 * width] = dk_ref[...].astype(jnp.bfloat16)
        out_ref[:, 2 * width : 3 * width] = dv_ref[...].astype(jnp.bfloat16)


def attention_specs(count, width):
    whole = pl.BlockSpec((count, width), lambda i: (0, 0))
    return [
        pl.BlockSpec(memory_space=pltpu.SMEM),
        pl.BlockSpec((count, 1), lambda i: (0, 0)),
        pl.BlockSpec((count, width), lambda i: (0, 0)),
        pl.BlockSpec((count, width), lambda i: (0, 1)),
        pl.BlockSpec((count, width), lambda i: (0, 2)),
    ], whole


def attend(projected, first, slopes, scale):
    count = projected.shape[0]
    width = projected.shape[1] // 3
    heads = width // HD
    window = min(LONGEST + BLOCK, count)
    specs, whole = attention_specs(count, width)
    area = heads * count * window
    return pl.pallas_call(
        functools.partial(attend_kernel, heads, window, scale),
        grid=(count // BLOCK,),
        in_specs=specs,
        out_specs=whole,
        out_shape=jax.ShapeDtypeStruct((count, width), jnp.bfloat16),
        compiler_params=pltpu.CompilerParams(vmem_limit_bytes=VMEM_LIMIT),
        cost_estimate=pl.CostEstimate(
            flops=4 * area * HD, bytes_accessed=8 * count * width, transcendentals=area
        ),
        name="attend",
    )(slopes, first, projected, projected, projected)


def attend_back(projected, first, slopes, scale, upstream):
    count = projected.shape[0]
    width = projected.shape[1] // 3
    heads = width // HD
    window = min(LONGEST + BLOCK, count)
    specs, whole = attention_specs(count, width)
    area = heads * count * window
    return pl.pallas_call(
        functools.partial(attend_back_kernel, heads, window, scale),
        grid=(count // BLOCK,),
        in_specs=specs + [whole],
        out_specs=pl.BlockSpec((count, 3 * width), lambda i: (0, 0)),
        out_shape=jax.ShapeDtypeStruct((count, 3 * width), jnp.bfloat16),
        scratch_shapes=[pltpu.VMEM((count, width), jnp.float32)] * 2,
        compiler_params=pltpu.CompilerParams(vmem_limit_bytes=VMEM_LIMIT),
        cost_estimate=pl.CostEstimate(
            flops=10 * area * HD, bytes_accessed=14 * count * width, transcendentals=area
        ),
        name="attend_back",
    )(slopes, first, projected, projected, projected, upstream)


def gather_group(shard):
    return lax.all_gather(shard, GROUP, axis=0, tiled=True)


def scatter_group(partial_sum):
    summed = lax.psum_scatter(
        partial_sum.astype(jnp.bfloat16), GROUP, scatter_dimension=0, tiled=True
    )
    return summed.astype(jnp.float32)


def take_columns(shard):
    return lax.all_to_all(shard, "col", split_axis=shard.ndim - 1, concat_axis=0, tiled=True)


def take_rows(shard):
    return lax.all_to_all(shard, "col", split_axis=0, concat_axis=1, tiled=True)


def gather_tokens(shard):
    rows, features = shard.shape
    cols = lax.axis_size("col")
    pieces = lax.all_gather(shard, GROUP, axis=0, tiled=False)
    pieces = pieces.reshape(lax.axis_size("row"), cols, rows, features)
    return pieces.transpose(0, 2, 1, 3).reshape(-1, cols * features)


def on_device(
    tokens,
    lengths,
    ln1_gain,
    ln1_bias,
    qkv_weight,
    qv_bias,
    out_weight,
    out_bias,
    ln2_gain,
    ln2_bias,
    up_weight,
    up_bias,
    down_weight,
    down_bias,
    cotangent,
):
    cols = lax.axis_size("col")
    rows = lax.axis_size("row")
    count = tokens.shape[0] * rows
    own = count // (rows * cols)
    place = lax.axis_index("row") * cols + lax.axis_index("col")
    local_heads = qkv_weight.shape[2] // cols // HD
    first_head = place * local_heads
    slopes = jnp.exp2(
        -8.0
        * (first_head + jnp.arange(local_heads, dtype=jnp.int32) + 1).astype(jnp.float32)
        / HEADS
    )
    scale = 1.0 / math.sqrt(HD)
    ends = jnp.cumsum(lengths[0])
    starts = ends - lengths[0]
    places = jnp.arange(count, dtype=jnp.int32)
    first = jnp.max(
        jnp.where(starts[None, :] <= places[:, None], starts[None, :], 0), axis=1, keepdims=True
    )

    vectors = jnp.stack([ln1_gain, ln1_bias, out_bias, ln2_gain, ln2_bias, down_bias])
    vectors = lax.all_gather(vectors, "col", axis=1, tiled=True)
    gain_one, shift_one, bias_out, gain_two, shift_two, bias_down = (vectors[i] for i in range(6))

    qkv_local = take_columns(qkv_weight).reshape(-1, 3 * local_heads * HD)
    out_local = take_rows(out_weight)
    up_local = take_columns(up_weight)
    down_local = take_rows(down_weight)

    all_tokens = gather_tokens(tokens)
    all_cotangent = gather_tokens(cotangent)

    def mine(array):
        return lax.dynamic_slice_in_dim(array, place * own, own, axis=0)

    centred_all, _ = norm_stats(all_tokens.astype(jnp.float32))
    normed_one = norm_apply(centred_all, gain_one, shift_one)
    residual = mine(all_tokens).astype(jnp.float32)
    upstream = mine(all_cotangent).astype(jnp.float32)
    bias_three = jnp.concatenate([qv_bias[0], jnp.zeros_like(qv_bias[0]), qv_bias[1]])
    projected = (product(normed_one, qkv_local) + bias_three.astype(jnp.float32)).astype(
        jnp.bfloat16
    )
    context = attend(projected, first, slopes, scale)
    attention_out = scatter_group(product(context, out_local))
    middle = residual + attention_out + bias_out.astype(jnp.float32)
    centred_two, inverse_two = norm_stats(middle)
    normed_two = gather_group(norm_apply(centred_two, gain_two, shift_two))
    hidden = product(normed_two, up_local) + up_bias.astype(jnp.float32)
    activated, gelu_pull = jax.vjp(gelu_tanh, hidden)
    activated = activated.astype(jnp.bfloat16)
    grad_active = product_flip(all_cotangent, down_local)
    grad_hidden = gelu_pull(grad_active)[0].astype(jnp.bfloat16)
    grad_normed_two = scatter_group(product_flip(grad_hidden, up_local))
    feed_out = scatter_group(product(activated, down_local))
    block_out = (middle + feed_out + bias_down.astype(jnp.float32)).astype(jnp.bfloat16)

    grad_up_bias = jnp.sum(grad_hidden.astype(jnp.float32), axis=0)
    grad_up = outer_sum(normed_two, grad_hidden).astype(jnp.bfloat16)
    grad_down = outer_sum(activated, all_cotangent).astype(jnp.bfloat16)
    grad_down_bias = jnp.sum(upstream, axis=0)

    back_two, grad_ln2_gain, grad_ln2_bias = norm_backward(
        grad_normed_two, centred_two, inverse_two, gain_two
    )
    grad_middle = upstream + back_two
    grad_out_bias = jnp.sum(grad_middle, axis=0)
    grad_attention = gather_group(grad_middle.astype(jnp.bfloat16))
    grad_context = product_flip(grad_attention, out_local).astype(jnp.bfloat16)
    grad_out = outer_sum(context, grad_attention).astype(jnp.bfloat16)
    grad_projected = attend_back(projected, first, slopes, scale, grad_context)
    summed = jnp.sum(grad_projected.astype(jnp.float32), axis=0).reshape(3, -1)
    grad_qv_bias = jnp.stack([summed[0], summed[2]])
    grad_normed_one = scatter_group(product_flip(grad_projected, qkv_local))
    grad_qkv = outer_sum(normed_one, grad_projected).astype(jnp.bfloat16)

    centred_one, inverse_one = norm_stats(residual)
    back_one, grad_ln1_gain, grad_ln1_bias = norm_backward(
        grad_normed_one, centred_one, inverse_one, gain_one
    )
    grad_tokens = grad_middle + back_one

    def to_columns(array):
        return lax.all_to_all(array, "col", split_axis=1, concat_axis=0, tiled=True)

    def dp_sum(array):
        return lax.psum(array.astype(jnp.bfloat16), "dp").astype(jnp.float32)

    grad_up_weight = dp_sum(lax.all_to_all(grad_up, "col", split_axis=0, concat_axis=1, tiled=True))
    grad_down_weight = dp_sum(to_columns(grad_down))
    grad_out_weight = dp_sum(to_columns(grad_out))
    width = local_heads * HD
    grad_qkv_weight = dp_sum(
        lax.all_to_all(
            grad_qkv.reshape(-1, 3, width), "col", split_axis=0, concat_axis=2, tiled=True
        )
    )
    biases = jnp.concatenate([grad_qv_bias.reshape(-1), grad_up_bias])
    biases = lax.psum(biases, "dp")
    vector_sums = lax.psum(
        jnp.stack(
            [grad_ln1_gain, grad_ln1_bias, grad_out_bias, grad_ln2_gain, grad_ln2_bias, grad_down_bias]
        ),
        ("dp", "row", "col"),
    )
    features = tokens.shape[1]
    vector_sums = lax.dynamic_slice_in_dim(
        vector_sums, lax.axis_index("col") * features, features, axis=1
    )
    return (
        to_columns(block_out),
        to_columns(grad_tokens),
        vector_sums[0],
        vector_sums[1],
        grad_qkv_weight,
        biases[: 2 * width].reshape(2, width),
        grad_out_weight,
        vector_sums[2],
        vector_sums[3],
        vector_sums[4],
        grad_up_weight,
        biases[2 * width :],
        grad_down_weight,
        vector_sums[5],
    )


def solution(mesh):
    return jax.shard_map(
        on_device,
        mesh=mesh,
        in_specs=(
            P(("dp", "row"), "col"),
            P("dp", None),
            P("col"),
            P("col"),
            P("col", None, "row"),
            P(None, ("row", "col")),
            P("row", "col"),
            P("col"),
            P("col"),
            P("col"),
            P("col", "row"),
            P(("row", "col")),
            P("row", "col"),
            P("col"),
            P(("dp", "row"), "col"),
        ),
        out_specs=(
            P(("dp", "row"), "col"),
            P(("dp", "row"), "col"),
            P("col"),
            P("col"),
            P("col", None, "row"),
            P(None, ("row", "col")),
            P("row", "col"),
            P("col"),
            P("col"),
            P("col"),
            P("col", "row"),
            P(("row", "col")),
            P("row", "col"),
            P("col"),
        ),
        check_vma=False,
    )
```

time: 1140 us -> 725 us (0.64)
  waiting for transfers between devices: 807 us -> 366 us
  matrix products: 123 us -> 55.4 us
  starting transfers between devices: 1.72 us -> 34.5 us
  Pallas kernels: 0 us -> 32.1 us
  blocking collectives: 64.3 us -> 79 us
    reduce_scatter x8 -> x4, waiting for transfers between devices: 480 us -> 139 us  [scatter_group(): lax.psum_scatter(partial_sum.astype(jnp.bfloat16), GROUP, scatter_dimensi...]
    all_gather x8 -> x4, waiting for transfers between devices: 229 us -> 63.4 us  [the longest x2 59.3 us: gather_group(): return lax.all_gather(shard, GROUP, axis=0, tiled=True)]
    all_to_all x0 -> x9, waiting for transfers between devices: none -> 73.2 us  [the longest x1 20.8 us: take_columns(): lax.all_to_all(shard, 'col', split_axis=shard.ndim - 1, concat_axis=0, ti...]
    dot_general x32 -> x8, matrix products: 101 us -> 34.9 us  [the longest x4 18 us: product(): return jnp.dot(left, right, preferred_element_type=jnp.float32)]
    all_to_all x0 -> x9, starting transfers between devices: none -> 34 us  [the longest x4 14.2 us: to_columns(): return lax.all_to_all(array, 'col', split_axis=1, concat_axis=0, tiled=True)]
    pallas_call x0 -> x2, Pallas kernels: none -> 32.1 us  [the longest x1 19.1 us: attend_back(): pl.pallas_call(functools.partial(attend_back_kernel, heads, window, scale...]
    reduce_sum x9 -> x5, other arithmetic: 14.4 us -> 41.4 us  [the longest x1 29.7 us: norm_stats(): inverse = lax.rsqrt(jnp.mean(away * away, axis=-1, keepdims=True) + epsilon)]
    all_to_all x0 -> x1, blocking collectives: none -> 21.9 us  [take_columns(): lax.all_to_all(shard, 'col', split_axis=shard.ndim - 1, concat_axis=0, ti...]
  transfers between devices with their start and end apart: 17 -> 18, of which waited for: 17 -> 14; matrix products, arithmetic and copies ran while one was open for 9% -> 13% of each run, Pallas kernels for 0% -> 0%
where the time goes in v1:
time: 725 us; the launch traced here: 718 us
  waiting for transfers between devices  366 us (50%)
  other arithmetic  80.6 us (11%)
  blocking collectives  79 us (11%)
  local copies, waits for them, and re-layouts  55.8 us (8%)
  matrix products  55.4 us (8%)
  starting transfers between devices  34.5 us (5%)
  Pallas kernels  32.1 us (4%)
  between operations  14.8 us (2%)
    reduce_scatter x4, waiting for transfers between devices, scatter_group(): lax.psum_scatter(partial_sum.astype(jnp.bfloat16), GROUP, scatter_dimensi...  139 us
    psum x1, waiting for transfers between devices, dp_sum(): return lax.psum(array.astype(jnp.bfloat16), 'dp').astype(jnp.float32)  88.4 us
    all_gather x2, waiting for transfers between devices, gather_group(): return lax.all_gather(shard, GROUP, axis=0, tiled=True)  59.3 us
    psum x1, blocking collectives, on_device(): lax.psum(jnp.stack([grad_ln1_gain, grad_ln1_bias, grad_out_bias, grad_ln2...  39.3 us
    reduce_sum x1, other arithmetic, norm_stats(): inverse = lax.rsqrt(jnp.mean(away * away, axis=-1, keepdims=True) + epsilon)  29.7 us
    all_to_all x1, blocking collectives, take_columns(): lax.all_to_all(shard, 'col', split_axis=shard.ndim - 1, concat_axis=0, ti...  21.9 us
    unnamed x54, local copies, waits for them, and re-layouts  21.2 us
    all_to_all x1, waiting for transfers between devices, take_columns(): lax.all_to_all(shard, 'col', split_axis=shard.ndim - 1, concat_axis=0, ti...  20.8 us
  transfers between devices with their start and end apart: 18, of which 14 were waited for; matrix products, arithmetic and copies ran while one was open for 13% of the time, Pallas kernels for 0%

profile of v1, /device:TPU:0, one launch (start us, length us, event | category | flops | bytes accessed | tf_op | source)
XLA Modules:
  0.0 718.0 jit_solution(11670669623430305248)
XLA Ops:
  29.7 20.8 %all-to-all-done = bf16[256,3,512]{0,1,2:T(4,128)(2,1)S(1)} async-done(((bf16[256,3,512]{0,1,2:T(4,128)(2,1)}), bf16[256,3,512]{0,1,2:T(4,128)(2,1)S(1)}, u32[]{:S(2)}, u32[]{:S(2)}) %all-to-all-start) | async-done | bytes 786464 | tf_op jit(solution)/shard_map/all_to_all | solution.py:192
  56.4 8.4 %convert_reduce_fusion = f32[2,1024]{1,0:T(2,128)S(1)} fusion(bf16[2,4,1024,256]{3,2,1,0:T(8,128)(2,1)} %bitcast.132), kind=kLoop, calls=%fused_computation.1 | loop fusion | flops 4192256 | bytes 4202496 | tf_op jit(solution)/shard_map/reduce_sum | solution.py:27
  64.8 29.7 %fusion.2 = f32[2,1024]{1,0:T(2,128)S(1)} fusion(f32[2,1024]{1,0:T(2,128)S(1)} %get-tuple-element.50, bf16[2,4,1024,256]{3,2,1,0:T(8,128)(2,1)S(1)} %bitcast.134), kind=kLoop, calls=%fused_computation.4 | loop fusion | flops 8386560 | bytes 4210688 | tf_op jit(solution)/shard_map/reduce_sum | solution.py:29
  94.5 17.7 %fusion.5 = bf16[2,1024,4,256]{3,2,1,0:T(4,128)(2,1)S(1)} fusion(f32[4,256]{1,0:T(4,128)S(1)} %add.166, f32[4,256]{1,0:T(4,128)S(1)} %mul.187, f32[2,1024]{1,0:T(2,128)S(1)} %get-tuple-element.52, f32[2,1024]{1,0:T(2,128)S(1)} %get-tuple-element.50, bf16[2,4,1024,256]{3,2,1,0:T(8,128)(2,1)S(1)} %bitcast.135), kind=kLoop, calls=%fused_computation.7 | loop fusion | flops 12582912 | bytes 8413184 | tf_op jit(solution)/shard_map/convert_element_type | solution.py:35
  115.7 13.0 %attend.1 = bf16[2048,128]{1,0:T(8,128)(2,1)S(1)} custom-call(f32[2]{0:T(128)S(1)} %multiply_exponential_fusion.slopes_ref, s32[2048,1]{1,0:T(8,128)S(1)} %copy.83.first_ref, bf16[2048,384]{1,0:T(8,128)(2,1)S(1)} %add_convert_fusion.2.q_ref.k_ref.v_ref, bf16[2048,384]{1,0:T(8,128)(2,1)S(1)} %add_convert_fusion.2.q_ref.k_ref.v_ref, ...), custom_call_target="tpu_custom_call" | custom-call | flops 805306368 | bytes 2097152 | tf_op jit(solution)/shard_map/attend/pallas_call | solution.py:144
  141.2 43.0 %reduce-scatter.5.cloned.1.call-done = bf16[256,1024]{1,0:T(8,128)(2,1)} async-done(((bf16[2048,1024]{1,0:T(8,128)(2,1)}), bf16[256,1024]{1,0:T(8,128)(2,1)}) %reduce-scatter.5.cloned.1.call-update) | async-done | bytes 524304 | tf_op jit(solution)/shard_map/reduce_scatter | solution.py:185
  191.9 21.9 %all_to_all.185 = bf16[256,4,512]{0,2,1:T(8,128)(2,1)} all-to-all(bf16[256,4,512]{0,2,1:T(8,128)(2,1)} %bitcast.160), channel_id=1, replica_groups=mesh['dp'=4,'row'=2,'col'=4] {'col'}, dimensions={1} | all-to-all | bytes 2097152 | tf_op jit(solution)/shard_map/all_to_all | solution.py:192
  220.6 15.7 %all-to-all-done.3 = bf16[4,512,256]{2,1,0:T(8,128)(2,1)} async-done(((bf16[4,512,256]{2,1,0:T(8,128)(2,1)}), bf16[4,512,256]{2,1,0:T(8,128)(2,1)}, u32[]{:S(2)}, u32[]{:S(2)}) %all-to-all-start.3) | async-done | bytes 1048608 | tf_op jit(solution)/shard_map/all_to_all | solution.py:196
  238.5 5.7 copy.89
  247.3 22.5 %all-gather.7.cloned.1.call-done = bf16[2048,1024]{1,0:T(8,128)(2,1)} async-done(((bf16[256,1024]{1,0:T(8,128)(2,1)}), bf16[2048,1024]{1,0:T(8,128)(2,1)}) %all-gather.7.cloned.1.call-update) | async-done | bytes 4194320 | tf_op jit(solution)/shard_map/all_gather | solution.py:181
  285.6 7.4 %convolution_convert_fusion.2 = bf16[2048,1024]{1,0:T(8,128)(2,1)} fusion(bf16[512,1024]{0,1:T(8,128)(2,1)} %bitcast.170, f32[2048,512]{1,0:T(8,128)} %copy-done.22, f32[512]{0:T(512)S(1)} %convert_element_type.140), kind=kOutput, calls=%fused_computation.27 | convolution fusion | flops 2160066560 | bytes 9439232 | tf_op jit(solution)/shard_map/dot_general | solution.py:47
  293.1 43.8 %reduce-scatter.9.cloned.1.call-done = bf16[256,1024]{1,0:T(8,128)(2,1)} async-done(((bf16[2048,1024]{1,0:T(8,128)(2,1)}), bf16[256,1024]{1,0:T(8,128)(2,1)}) %reduce-scatter.9.cloned.1.call-update) | async-done | bytes 524304 | tf_op jit(solution)/shard_map/reduce_scatter | solution.py:185
  339.1 52.3 %reduce-scatter.7.cloned.1.call-done = bf16[256,1024]{1,0:T(8,128)(2,1)} async-done(((bf16[2048,1024]{1,0:T(8,128)(2,1)}), bf16[256,1024]{1,0:T(8,128)(2,1)}) %reduce-scatter.7.cloned.1.call-update) | async-done | bytes 524304 | tf_op jit(solution)/shard_map/reduce_scatter | solution.py:185
  396.5 36.8 %all-gather.9.cloned.1.call-done = bf16[2048,1024]{1,0:T(8,128)(2,1)} async-done(((bf16[256,1024]{1,0:T(8,128)(2,1)}), bf16[2048,1024]{1,0:T(8,128)(2,1)}) %all-gather.9.cloned.1.call-update) | async-done | bytes 4194320 | tf_op jit(solution)/shard_map/all_gather | solution.py:181
  436.8 19.1 %attend_back.1 = bf16[2048,384]{1,0:T(8,128)(2,1)S(1)} custom-call(f32[2]{0:T(128)S(1)} %multiply_exponential_fusion.slopes_ref, s32[2048,1]{1,0:T(8,128)S(1)} %copy.83.first_ref, bf16[2048,384]{1,0:T(8,128)(2,1)S(1)} %add_convert_fusion.2.q_ref.k_ref.v_ref, bf16[2048,384]{1,0:T(8,128)(2,1)S(1)} %add_convert_fusion.2.q_ref.k_ref.v_ref, ...), custom_call_target="tpu_custom_call" | custom-call | flops 2013265920 | bytes 3670016 | tf_op jit(solution)/shard_map/attend_back/pallas_call | solution.py:165
  462.9 5.5 convolution_convert_fusion.6
  471.9 6.6 convolution_convert_fusion.5
  479.6 7.6 %all-to-all-done.8 = bf16[4,256,512]{2,1,0:T(8,128)(2,1)S(1)} async-done(((bf16[4,256,512]{2,1,0:T(8,128)(2,1)}), bf16[4,256,512]{2,1,0:T(8,128)(2,1)S(1)}, u32[]{:S(2)}, u32[]{:S(2)}) %all-to-all-start.8) | async-done | bytes 1048608 | tf_op jit(solution)/shard_map/all_to_all | solution.py:312
  499.8 9.1 %all-to-all-done.9 = bf16[512,4,256]{2,0,1:T(8,128)(2,1)S(1)} async-done(((bf16[512,4,256]{2,0,1:T(8,128)(2,1)}), bf16[512,4,256]{2,0,1:T(8,128)(2,1)S(1)}, u32[]{:S(2)}, u32[]{:S(2)}) %all-to-all-start.9) | async-done | bytes 1048608 | tf_op jit(solution)/shard_map/all_to_all | solution.py:307
  516.9 10.8 %all-to-all-done.6 = bf16[1024,3,128]{2,1,0:T(4,128)(2,1)} async-done(((bf16[1024,3,128]{2,1,0:T(4,128)(2,1)}), bf16[1024,3,128]{2,1,0:T(4,128)(2,1)}, u32[]{:S(2)}, u32[]{:S(2)}) %all-to-all-start.6) | async-done | bytes 786464 | tf_op jit(solution)/shard_map/all_to_all | solution.py:317
  542.2 8.8 %all-to-all-done.4 = bf16[256,4,256]{2,0,1:T(8,128)(2,1)S(1)} async-done(((bf16[256,4,256]{2,0,1:T(8,128)(2,1)}), bf16[256,4,256]{2,0,1:T(8,128)(2,1)S(1)}, u32[]{:S(2)}, u32[]{:S(2)}) %all-to-all-start.4) | async-done | bytes 524320 | tf_op jit(solution)/shard_map/all_to_all | solution.py:307
  559.3 12.4 %psum.44 = f32[768]{0:T(1024)S(1)} all-reduce(f32[768]{0:T(1024)S(1)} %pad_maximum_fusion), channel_id=1, replica_groups=mesh['dp'=4,'row'=2,'col'=4] {'dp'}, use_global_device_ids=true, to_apply=%region_26.27 | all-reduce | flops 768 | bytes 6144 | tf_op jit(solution)/shard_map/psum | solution.py:322
  572.9 88.4 %all-reduce.3.cloned.1.call-done = (bf16[256,3,512]{2,0,1:T(8,128)(2,1)}, bf16[512,256]{1,0:T(8,128)(2,1)}, bf16[256,2048]{1,0:T(8,128)(2,1)}, bf16[2048,256]{1,0:T(8,128)(2,1)}) async-done(((bf16[256,3,512]{2,0,1:T(8,128)(2,1)}, bf16[512,256]{1,0:T(8,128)(2,1)}, bf16[256,2048]{1,0:T(8,128)(2,1)}, bf16[2048,256]{1,0:T(8,128)(2,1)}), (bf16[256,3,512]{2,0,1:T(8,128)(2,1)}, bf16[512,256]{1,0:T(8,128)(2,1)}, ...) | async-done | bytes 3145744 | tf_op jit(solution)/shard_map/psum | solution.py:310
  669.2 39.3 %psum.42 = f32[6,1024]{1,0:T(8,128)S(1)} all-reduce(f32[6,1024]{1,0:T(8,128)S(1)} %stack.58), channel_id=1, replica_groups=mesh['dp'=4,'row'=2,'col'=4] {'dp','row','col'}, use_global_device_ids=true, to_apply=%region_22.23 | all-reduce | flops 6144 | bytes 49152 | tf_op jit(solution)/shard_map/psum | solution.py:323
  (160 shorter events, 156.8 us)
Async XLA Ops:
  7.2 22.3 %copy-start.18 = (bf16[2,128]{1,0:T(2,128)(2,1)S(1)}, bf16[2,128]{1,0:T(2,128)(2,1)}, u32[]{:S(2)}) copy-start(bf16[2,128]{1,0:T(2,128)(2,1)} %param.20) | copy-start | bytes 1540
  7.2 49.2 %all-gather.11.cloned.1.call-start = ((), (), s32[]{:S(2)}) async-start(), calls=%async_computation.20 | async-start | bytes 4718592 | tf_op jit(solution)/shard_map/all_gather | solution.py:202
  7.9 17.4 %all-to-all-start.1 = ((bf16[4,128,256]{2,1,0:T(8,128)(2,1)}), bf16[4,128,256]{2,1,0:T(8,128)(2,1)S(1)}, u32[]{:S(2)}, u32[]{:S(2)}) async-start(bf16[4,128,256]{2,1,0:T(8,128)(2,1)} %bitcast.179), calls=%async_computation.1 | async-start | bytes 524288 | tf_op jit(solution)/shard_map/all_to_all | solution.py:196
  25.4 25.2 %all-to-all-start = ((bf16[256,3,512]{0,1,2:T(4,128)(2,1)}), bf16[256,3,512]{0,1,2:T(4,128)(2,1)S(1)}, u32[]{:S(2)}, u32[]{:S(2)}) async-start(bf16[256,3,512]{0,1,2:T(4,128)(2,1)} %copy.81), calls=%async_computation | async-start | bytes 2097152 | tf_op jit(solution)/shard_map/all_to_all | solution.py:192
  28.9 155.4 %reduce-scatter.5.cloned.1.call-start = ((), (), s32[]{:S(2)}) async-start(), calls=%async_computation.14 | async-start | bytes 4718592 | tf_op jit(solution)/shard_map/reduce_scatter | solution.py:185
  132.0 106.5 %all-gather.13.cloned.1.call-start = ((), (), s32[]{:S(2)}) async-start(), calls=%async_computation.21 | async-start | bytes 4718592 | tf_op jit(solution)/shard_map/all_gather | solution.py:202
  132.7 137.1 %all-gather.7.cloned.1.call-start = ((), (), s32[]{:S(2)}) async-start(), calls=%async_computation.15 | async-start | bytes 4718592 | tf_op jit(solution)/shard_map/all_gather | solution.py:181
  187.3 30.8 %copy-start.19 = (bf16[512]{0:T(512)(128)(2,1)S(1)}, bf16[512]{0:T(512)(128)(2,1)}, u32[]{:S(2)}) copy-start(bf16[512]{0:T(512)(128)(2,1)} %param.26) | copy-start | bytes 3076
  213.8 22.4 %all-to-all-start.3 = ((bf16[4,512,256]{2,1,0:T(8,128)(2,1)}), bf16[4,512,256]{2,1,0:T(8,128)(2,1)}, u32[]{:S(2)}, u32[]{:S(2)}) async-start(bf16[4,512,256]{2,1,0:T(8,128)(2,1)} %bitcast.169), calls=%async_computation.4 | async-start | bytes 2097152 | tf_op jit(solution)/shard_map/all_to_all | solution.py:196
  218.1 118.8 %reduce-scatter.9.cloned.1.call-start = ((), (), s32[]{:S(2)}) async-start(), calls=%async_computation.17 | async-start | bytes 4718592 | tf_op jit(solution)/shard_map/reduce_scatter | solution.py:185
  285.4 106.1 %reduce-scatter.7.cloned.1.call-start = ((), (), s32[]{:S(2)}) async-start(), calls=%async_computation.16 | async-start | bytes 4718592 | tf_op jit(solution)/shard_map/reduce_scatter | solution.py:185
  293.0 140.3 %all-gather.9.cloned.1.call-start = ((), (), s32[]{:S(2)}) async-start(), calls=%async_computation.18 | async-start | bytes 4718592 | tf_op jit(solution)/shard_map/all_gather | solution.py:181
  396.5 154.8 %reduce-scatter.11.cloned.1.call-start = ((), (), s32[]{:S(2)}) async-start(), calls=%async_computation.19 | async-start | bytes 4718592 | tf_op jit(solution)/shard_map/reduce_scatter | solution.py:185
  436.8 20.2 %copy-start.15 = (bf16[48,8,4,256]{3,1,2,0:T(8,128)(2,1)S(1)}, bf16[48,8,4,256]{3,1,2,0:T(8,128)(2,1)}, u32[]{:S(2)}) copy-start(bf16[48,8,4,256]{3,1,2,0:T(8,128)(2,1)} %copy.104) | copy-start | bytes 2359300
  468.4 18.8 %all-to-all-start.8 = ((bf16[4,256,512]{2,1,0:T(8,128)(2,1)}), bf16[4,256,512]{2,1,0:T(8,128)(2,1)S(1)}, u32[]{:S(2)}, u32[]{:S(2)}) async-start(bf16[4,256,512]{2,1,0:T(8,128)(2,1)} %bitcast.49), calls=%async_computation.12 | async-start | bytes 2097152 | tf_op jit(solution)/shard_map/all_to_all | solution.py:312
  488.1 20.8 %all-to-all-start.9 = ((bf16[512,4,256]{2,0,1:T(8,128)(2,1)}), bf16[512,4,256]{2,0,1:T(8,128)(2,1)S(1)}, u32[]{:S(2)}, u32[]{:S(2)}) async-start(bf16[512,4,256]{2,0,1:T(8,128)(2,1)} %bitcast.157), calls=%async_computation.13 | async-start | bytes 2097152 | tf_op jit(solution)/shard_map/all_to_all | solution.py:307
  508.9 24.6 %copy-start.6 = (bf16[512,4,256]{2,0,1:T(8,128)(2,1)}, bf16[512,4,256]{2,0,1:T(8,128)(2,1)S(1)}, u32[]{:S(2)}) copy-start(bf16[512,4,256]{2,0,1:T(8,128)(2,1)S(1)} %all-to-all-done.9) | copy-start | bytes 3145732
  508.9 18.8 %all-to-all-start.6 = ((bf16[1024,3,128]{2,1,0:T(4,128)(2,1)}), bf16[1024,3,128]{2,1,0:T(4,128)(2,1)}, u32[]{:S(2)}, u32[]{:S(2)}) async-start(bf16[1024,3,128]{2,1,0:T(4,128)(2,1)} %copy.92), calls=%async_computation.10 | async-start | bytes 2097152 | tf_op jit(solution)/shard_map/all_to_all | solution.py:317
  527.7 9.4 %all-to-all-start.7 = ((bf16[128,4,256]{2,0,1:T(8,128)(2,1)}), bf16[128,4,256]{2,0,1:T(8,128)(2,1)S(1)}, u32[]{:S(2)}, u32[]{:S(2)}) async-start(bf16[128,4,256]{2,0,1:T(8,128)(2,1)} %bitcast.131), calls=%async_computation.11 | async-start | bytes 524288 | tf_op jit(solution)/shard_map/all_to_all | solution.py:307
  531.1 130.3 %all-reduce.3.cloned.1.call-start = ((), (), s32[]{:S(2)}) async-start(), calls=%async_computation.22 | async-start | bytes 6291456 | tf_op jit(solution)/shard_map/psum | solution.py:310
  536.7 16.4 %copy-start.4 = (f32[256,1024]{1,0:T(8,128)S(1)}, f32[256,1024]{1,0:T(8,128)}, u32[]{:S(2)}) copy-start(f32[256,1024]{1,0:T(8,128)} %copy-done.3) | copy-start | bytes 3145732
  538.7 12.3 %all-to-all-start.4 = ((bf16[256,4,256]{2,0,1:T(8,128)(2,1)}), bf16[256,4,256]{2,0,1:T(8,128)(2,1)S(1)}, u32[]{:S(2)}, u32[]{:S(2)}) async-start(bf16[256,4,256]{2,0,1:T(8,128)(2,1)} %bitcast.164), calls=%async_computation.6 | async-start | bytes 1048576 | tf_op jit(solution)/shard_map/all_to_all | solution.py:307
  555.8 153.4 %all-to-all-start.5 = ((f32[256,4,256]{2,0,1:T(8,128)}), f32[256,4,256]{2,0,1:T(8,128)S(1)}, u32[]{:S(2)}, u32[]{:S(2)}) async-start(f32[256,4,256]{2,0,1:T(8,128)} %bitcast.129), calls=%async_computation.9 | async-start | bytes 2097152 | tf_op jit(solution)/shard_map/all_to_all | solution.py:307
  661.4 47.9 %copy-start.10 = (bf16[256,4,256]{2,0,1:T(8,128)(2,1)S(1)}, bf16[256,4,256]{2,0,1:T(8,128)(2,1)}, u32[]{:S(2)}) copy-start(bf16[256,4,256]{2,0,1:T(8,128)(2,1)} %copy-done.9) | copy-start | bytes 1572868
  (17 other events, 74.9 us)
Sparse Core Ops, SparseCore 0:
  9.9 46.4 all-gather.10
  132.1 52.0 reduce-scatter.4
  186.3 43.9 all-gather.12
  232.8 37.0 all-gather.6
  285.5 51.3 reduce-scatter.8
  340.1 51.3 reduce-scatter.6
  396.6 36.6 all-gather.8
  461.4 54.1 reduce-scatter.10
  537.9 123.3 all-reduce.2

commit v2 on v1

--- a/solution.py
+++ b/solution.py
@@ -177,31 +177,363 @@
     )(slopes, first, projected, projected, projected, upstream)
 
 
-def gather_group(shard):
-    return lax.all_gather(shard, GROUP, axis=0, tiled=True)
+MESH = pl.DeviceIdType.MESH
+MOVE = pl.CostEstimate(flops=0, bytes_accessed=64 * 1024 * 1024, transcendentals=0)
+ROWS = 2
+COLS = 4
+
+
+def positions():
+    row = lax.axis_index("row")
+    col = lax.axis_index("col")
+    return row, col, 1 - row, lax.rem(col + 2, COLS), col + 1 - 2 * lax.rem(col, 2)
+
+
+def greet(devices):
+    barrier = pltpu.get_barrier_semaphore()
+    for device in devices:
+        pl.semaphore_signal(barrier, inc=1, device_id=device, device_id_type=MESH)
+    pl.semaphore_wait(barrier, len(devices))
+
+
+def remote(source, target, send_sem, recv_sem, device):
+    return pltpu.make_async_remote_copy(
+        src_ref=source,
+        dst_ref=target,
+        send_sem=send_sem,
+        recv_sem=recv_sem,
+        device_id=device,
+        device_id_type=MESH,
+    )
+
+
+GATHER_COPIES = 11
+
+
+def gather_kernel(tiled, total, *refs):
+    ins = refs[:total]
+    outs = refs[total : 2 * total]
+    local_sem, send_sem, recv_sem = refs[2 * total :]
+    row, col, other_row, other_col, twin = positions()
+    side, over, core = {"row": other_row}, {"col": other_col}, {"col": twin}
+    greet([side, over, core])
+    copies = []
+    locals_ = []
+    for which in range(total):
+        block, out = ins[which], outs[which]
+        count, width = block.shape
+        half = count // 2
+
+        def place(r, c, low, size, out=out, count=count, width=width):
+            if tiled:
+                at = pl.multiple_of(c * width, width)
+                return out.at[pl.ds(pl.multiple_of(r * count, count) + low, size), pl.ds(at, width)]
+            at = pl.multiple_of((r * COLS + c) * count, count)
+            return out.at[pl.ds(at + low, size), :]
+
+        def mine(low, size, block=block):
+            return block.at[pl.ds(low, size), :]
+
+        def one(index, source, target, device, base=which * GATHER_COPIES):
+            return remote(source, target, send_sem.at[base + index], recv_sem.at[base + index], device)
+
+        def relay(index, r, c, low, size, device):
+            return one(index, place(r, c, low, size), place(r, c, low, size), device)
+
+        copies.append(
+            [
+                one(0, mine(0, half), place(row, col, 0, half), side),
+                one(1, mine(half, half), place(row, col, half, half), over),
+                one(2, mine(half, half), place(row, col, half, half), side),
+                one(3, mine(0, half), place(row, col, 0, half), over),
+                one(4, mine(0, count), place(row, col, 0, count), core),
+                relay(5, other_row, col, 0, half, over),
+                relay(6, row, other_col, half, half, side),
+                relay(7, other_row, col, 0, count, core),
+                relay(8, row, other_col, 0, count, core),
+                relay(9, other_row, other_col, 0, half, core),
+                relay(10, other_row, other_col, half, half, core),
+            ]
+        )
+        locals_.append(
+            pltpu.make_async_copy(block, place(row, col, 0, count), local_sem.at[which])
+        )
+        for index in range(5):
+            copies[which][index].start()
+        locals_[which].start()
+    for which in range(total):
+        group = copies[which]
+        group[0].wait_recv()
+        group[5].start()
+        group[1].wait_recv()
+        group[6].start()
+        group[2].wait_recv()
+        group[7].start()
+        group[3].wait_recv()
+        group[8].start()
+    for which in range(total):
+        group = copies[which]
+        group[5].wait_recv()
+        group[9].start()
+        group[6].wait_recv()
+        group[10].start()
+    for which in range(total):
+        for index in (4, 7, 8, 9, 10):
+            copies[which][index].wait_recv()
+        for index in range(GATHER_COPIES):
+            copies[which][index].wait_send()
+        locals_[which].wait()
+
+
+def gather_group(shards, tiled, collective_id):
+    total = len(shards)
+    shapes = []
+    for shard in shards:
+        count, width = shard.shape
+        shape = (ROWS * count, COLS * width) if tiled else (ROWS * COLS * count, width)
+        shapes.append(jax.ShapeDtypeStruct(shape, shard.dtype))
+    return pl.pallas_call(
+        functools.partial(gather_kernel, tiled, total),
+        in_specs=[pl.BlockSpec(memory_space=pltpu.VMEM)] * total,
+        out_specs=[pl.BlockSpec(memory_space=pltpu.VMEM)] * total,
+        out_shape=shapes,
+        scratch_shapes=[
+            pltpu.SemaphoreType.DMA((total,)),
+            pltpu.SemaphoreType.DMA((total * GATHER_COPIES,)),
+            pltpu.SemaphoreType.DMA((total * GATHER_COPIES,)),
+        ],
+        compiler_params=pltpu.CompilerParams(
+            collective_id=collective_id, has_side_effects=True, vmem_limit_bytes=VMEM_LIMIT
+        ),
+        cost_estimate=MOVE,
+        name="gather_group",
+    )(*shards)
+
+
+def scatter_kernel(part_ref, out_ref, pair, work, from_side, from_over, last, passed, send_sem, recv_sem):
+    own = out_ref.shape[0]
+    half = own // 2
+    row, col, other_row, other_col, twin = positions()
+    side, over, core = {"row": other_row}, {"col": other_col}, {"col": twin}
+    other_twin = lax.rem(twin + 2, COLS)
+    low, high = pl.ds(0, half), pl.ds(half, half)
+    keep = [(other_row, other_col), (other_row, col), (row, other_col), (row, col)]
+    give = [(other_row, other_twin), (other_row, twin), (row, other_twin), (row, twin)]
+
+    def piece(r, c):
+        return part_ref.at[pl.ds(pl.multiple_of((r * COLS + c) * own, own), own), :]
+
+    def one(index, source, target, device):
+        return remote(source, target, send_sem.at[index], recv_sem.at[index], device)
+
+    greet([side, over, core])
+    first = [one(chip, piece(*give[chip]), pair.at[chip], core) for chip in range(4)]
+    for copy in first:
+        copy.start()
+    diag_side = one(4, work.at[0, low], from_side.at[0], side)
+    near_side = one(5, work.at[1, low], from_side.at[1], side)
+    diag_over = one(6, work.at[0, high], from_over.at[0], over)
+    near_over = one(7, work.at[2, high], from_over.at[1], over)
+    last_over = one(8, passed.at[0], last.at[0], over)
+    last_side = one(9, passed.at[1], last.at[1], side)
+
+    def add_pair(chip):
+        first[chip].wait_recv()
+        kept = piece(*keep[chip])[...].astype(jnp.float32)
+        work[chip] = (kept + pair[chip].astype(jnp.float32)).astype(jnp.bfloat16)
+
+    add_pair(0)
+    diag_side.start()
+    diag_over.start()
+    add_pair(1)
+    near_side.start()
+    add_pair(2)
+    near_over.start()
+    add_pair(3)
+    diag_side.wait_recv()
+    passed[0] = (work[2, low].astype(jnp.float32) + from_side[0].astype(jnp.float32)).astype(
+        jnp.bfloat16
+    )
+    last_over.start()
+    diag_over.wait_recv()
+    passed[1] = (work[1, high].astype(jnp.float32) + from_over[0].astype(jnp.float32)).astype(
+        jnp.bfloat16
+    )
+    last_side.start()
+    near_side.wait_recv()
+    out_ref[low, :] = work[3, low].astype(jnp.float32) + from_side[1].astype(jnp.float32)
+    near_over.wait_recv()
+    out_ref[high, :] = work[3, high].astype(jnp.float32) + from_over[1].astype(jnp.float32)
+    last_over.wait_recv()
+    out_ref[low, :] += last[0].astype(jnp.float32)
+    last_side.wait_recv()
+    out_ref[high, :] += last[1].astype(jnp.float32)
+    for copy in first + [diag_side, near_side, diag_over, near_over, last_over, last_side]:
+        copy.wait_send()
 
 
 def scatter_group(partial_sum):
-    summed = lax.psum_scatter(
-        partial_sum.astype(jnp.bfloat16), GROUP, scatter_dimension=0, tiled=True
-    )
-    return summed.astype(jnp.float32)
-
-
-def take_columns(shard):
-    return lax.all_to_all(shard, "col", split_axis=shard.ndim - 1, concat_axis=0, tiled=True)
-
-
-def take_rows(shard):
-    return lax.all_to_all(shard, "col", split_axis=0, concat_axis=1, tiled=True)
-
-
-def gather_tokens(shard):
-    rows, features = shard.shape
-    cols = lax.axis_size("col")
-    pieces = lax.all_gather(shard, GROUP, axis=0, tiled=False)
-    pieces = pieces.reshape(lax.axis_size("row"), cols, rows, features)
-    return pieces.transpose(0, 2, 1, 3).reshape(-1, cols * features)
+    count, width = partial_sum.shape
+    own = count // (ROWS * COLS)
+    half = own // 2
+    return pl.pallas_call(
+        scatter_kernel,
+        in_specs=[pl.BlockSpec(memory_space=pltpu.VMEM)],
+        out_specs=pl.BlockSpec(memory_space=pltpu.VMEM),
+        out_shape=jax.ShapeDtypeStruct((own, width), jnp.float32),
+        scratch_shapes=[
+            pltpu.VMEM((4, own, width), jnp.bfloat16),
+            pltpu.VMEM((4, own, width), jnp.bfloat16),
+            pltpu.VMEM((2, half, width), jnp.bfloat16),
+            pltpu.VMEM((2, half, width), jnp.bfloat16),
+            pltpu.VMEM((2, half, width), jnp.bfloat16),
+            pltpu.VMEM((2, half, width), jnp.bfloat16),
+            pltpu.SemaphoreType.DMA((10,)),
+            pltpu.SemaphoreType.DMA((10,)),
+        ],
+        compiler_params=pltpu.CompilerParams(
+            collective_id=2, has_side_effects=True, vmem_limit_bytes=VMEM_LIMIT
+        ),
+        cost_estimate=MOVE,
+        name="scatter_group",
+    )(partial_sum.astype(jnp.bfloat16))
+
+
+def exchange_copies(plan, ins, outs, local_sem, send_sem, recv_sem):
+    col = lax.axis_index("col")
+    copies = []
+    locals_ = []
+    index = 0
+    local = 0
+    for kind, groups, source, target in zip(*zip(*plan), ins, outs):
+        for group in range(groups):
+            for step in range(COLS):
+                peer = lax.rem(col + step, COLS)
+                if kind == "columns":
+                    rows, width = source.shape[0], target.shape[1] // groups
+                    away = pl.multiple_of((group * COLS + peer) * width, width)
+                    block = source.at[:, pl.ds(away, width)]
+                    slot = target.at[
+                        pl.ds(pl.multiple_of(col * rows, rows), rows), pl.ds(group * width, width)
+                    ]
+                else:
+                    rows, width = target.shape[0], source.shape[1] // groups
+                    away = pl.multiple_of(peer * rows, rows)
+                    block = source.at[pl.ds(away, rows), pl.ds(group * width, width)]
+                    slot = target.at[
+                        :, pl.ds(pl.multiple_of((group * COLS + col) * width, width), width)
+                    ]
+                if step == 0:
+                    locals_.append(pltpu.make_async_copy(block, slot, local_sem.at[local]))
+                    local += 1
+                else:
+                    copies.append(
+                        remote(block, slot, send_sem.at[index], recv_sem.at[index], {"col": peer})
+                    )
+                    index += 1
+    return copies, locals_
+
+
+def greet_columns():
+    col = lax.axis_index("col")
+    greet([{"col": lax.rem(col + step, COLS)} for step in range(1, COLS)])
+
+
+def exchange_kernel(plan, *refs):
+    total = len(plan)
+    greet_columns()
+    copies, locals_ = exchange_copies(plan, refs[:total], refs[total : 2 * total], *refs[2 * total :])
+    for copy in copies + locals_:
+        copy.start()
+    for copy in copies + locals_:
+        copy.wait()
+
+
+def exchange_shapes(arrays, plan):
+    shapes = []
+    for array, (kind, _) in zip(arrays, plan):
+        rows, width = array.shape
+        shape = (rows * COLS, width // COLS) if kind == "columns" else (rows // COLS, width * COLS)
+        shapes.append(jax.ShapeDtypeStruct(shape, array.dtype))
+    blocks = sum(groups for _, groups in plan)
+    scratch = [
+        pltpu.SemaphoreType.DMA((blocks,)),
+        pltpu.SemaphoreType.DMA((blocks * (COLS - 1),)),
+        pltpu.SemaphoreType.DMA((blocks * (COLS - 1),)),
+    ]
+    return shapes, scratch
+
+
+def exchange(arrays, plan, collective_id):
+    shapes, scratch = exchange_shapes(arrays, plan)
+    return pl.pallas_call(
+        functools.partial(exchange_kernel, plan),
+        in_specs=[pl.BlockSpec(memory_space=pl.ANY)] * len(arrays),
+        out_specs=[pl.BlockSpec(memory_space=pl.ANY)] * len(arrays),
+        out_shape=shapes,
+        scratch_shapes=scratch,
+        compiler_params=pltpu.CompilerParams(
+            collective_id=collective_id, has_side_effects=True, vmem_limit_bytes=VMEM_LIMIT
+        ),
+        cost_estimate=MOVE,
+        name="exchange",
+    )(*arrays)
+
+
+def total_kernel(groups, block_ref, out_ref, slots, local_sem, send_sem, recv_sem):
+    total = groups * ROWS
+    here = lax.axis_index("dp") * ROWS + lax.axis_index("row")
+    peers = []
+    for step in range(1, total):
+        peer = lax.rem(here + step, total)
+        peers.append({"dp": lax.div(peer, ROWS), "row": lax.rem(peer, ROWS)})
+    greet(peers)
+    own = pltpu.make_async_copy(block_ref, slots.at[here], local_sem)
+    own.start()
+    copies = [
+        remote(block_ref, slots.at[here], send_sem.at[index], recv_sem.at[index], peer)
+        for index, peer in enumerate(peers)
+    ]
+    for copy in copies:
+        copy.start()
+    own.wait()
+    for copy in copies:
+        copy.wait()
+    half = block_ref.shape[0] // 2
+    row = lax.axis_index("row")
+    upper = slots[0, :half]
+    for index in range(1, total):
+        upper = upper + slots[index, :half]
+    lower = slots[row, half:]
+    for index in range(1, groups):
+        lower = lower + slots[index * ROWS + row, half:]
+    out_ref[:half] = upper
+    out_ref[half:] = lower
+
+
+def total_over_rows(block):
+    groups = lax.axis_size("dp")
+    others = groups * ROWS - 1
+    return pl.pallas_call(
+        functools.partial(total_kernel, groups),
+        in_specs=[pl.BlockSpec(memory_space=pltpu.VMEM)],
+        out_specs=pl.BlockSpec(memory_space=pltpu.VMEM),
+        out_shape=jax.ShapeDtypeStruct(block.shape, block.dtype),
+        scratch_shapes=[
+            pltpu.VMEM((groups * ROWS, *block.shape), block.dtype),
+            pltpu.SemaphoreType.DMA,
+            pltpu.SemaphoreType.DMA((others,)),
+            pltpu.SemaphoreType.DMA((others,)),
+        ],
+        compiler_params=pltpu.CompilerParams(
+            collective_id=7, has_side_effects=True, vmem_limit_bytes=VMEM_LIMIT
+        ),
+        name="total_over_rows",
+    )(block)
+
+
+def after(array, *others):
+    return lax.optimization_barrier((array, *others))[0]
 
 
 def on_device(
@@ -245,13 +577,12 @@
     vectors = lax.all_gather(vectors, "col", axis=1, tiled=True)
     gain_one, shift_one, bias_out, gain_two, shift_two, bias_down = (vectors[i] for i in range(6))
 
-    qkv_local = take_columns(qkv_weight).reshape(-1, 3 * local_heads * HD)
-    out_local = take_rows(out_weight)
-    up_local = take_columns(up_weight)
-    down_local = take_rows(down_weight)
-
-    all_tokens = gather_tokens(tokens)
-    all_cotangent = gather_tokens(cotangent)
+    all_tokens, all_cotangent = gather_group([tokens, cotangent], True, 0)
+    qkv_local, out_local, up_local, down_local = exchange(
+        [qkv_weight.reshape(qkv_weight.shape[0], -1), out_weight, up_weight, down_weight],
+        (("columns", 3), ("rows", 1), ("columns", 1), ("rows", 1)),
+        3,
+    )
 
     def mine(array):
         return lax.dynamic_slice_in_dim(array, place * own, own, axis=0)
@@ -268,19 +599,19 @@
     attention_out = scatter_group(product(context, out_local))
     middle = residual + attention_out + bias_out.astype(jnp.float32)
     centred_two, inverse_two = norm_stats(middle)
-    normed_two = gather_group(norm_apply(centred_two, gain_two, shift_two))
+    normed_two = gather_group([norm_apply(centred_two, gain_two, shift_two)], False, 1)[0]
     hidden = product(normed_two, up_local) + up_bias.astype(jnp.float32)
     activated, gelu_pull = jax.vjp(gelu_tanh, hidden)
     activated = activated.astype(jnp.bfloat16)
     grad_active = product_flip(all_cotangent, down_local)
     grad_hidden = gelu_pull(grad_active)[0].astype(jnp.bfloat16)
-    grad_normed_two = scatter_group(product_flip(grad_hidden, up_local))
-    feed_out = scatter_group(product(activated, down_local))
-    block_out = (middle + feed_out + bias_down.astype(jnp.float32)).astype(jnp.bfloat16)
-
     grad_up_bias = jnp.sum(grad_hidden.astype(jnp.float32), axis=0)
     grad_up = outer_sum(normed_two, grad_hidden).astype(jnp.bfloat16)
     grad_down = outer_sum(activated, all_cotangent).astype(jnp.bfloat16)
+    grad_up, grad_down = exchange([grad_up, grad_down], (("rows", 1), ("columns", 1)), 4)
+    grad_up_weight, grad_down_weight = lax.psum((grad_up, grad_down), "dp")
+    partial_two = product_flip(grad_hidden, up_local).astype(jnp.bfloat16)
+    grad_normed_two = scatter_group(after(partial_two, grad_up, grad_down))
     grad_down_bias = jnp.sum(upstream, axis=0)
 
     back_two, grad_ln2_gain, grad_ln2_bias = norm_backward(
@@ -288,14 +619,24 @@
     )
     grad_middle = upstream + back_two
     grad_out_bias = jnp.sum(grad_middle, axis=0)
-    grad_attention = gather_group(grad_middle.astype(jnp.bfloat16))
+    grad_attention = gather_group([grad_middle.astype(jnp.bfloat16)], False, 1)[0]
     grad_context = product_flip(grad_attention, out_local).astype(jnp.bfloat16)
     grad_out = outer_sum(context, grad_attention).astype(jnp.bfloat16)
     grad_projected = attend_back(projected, first, slopes, scale, grad_context)
     summed = jnp.sum(grad_projected.astype(jnp.float32), axis=0).reshape(3, -1)
     grad_qv_bias = jnp.stack([summed[0], summed[2]])
-    grad_normed_one = scatter_group(product_flip(grad_projected, qkv_local))
     grad_qkv = outer_sum(normed_one, grad_projected).astype(jnp.bfloat16)
+    grad_out, grad_qkv = exchange([grad_out, grad_qkv], (("columns", 1), ("rows", 3)), 5)
+    sent_out, sent_qkv, grad_up_weight, grad_down_weight = lax.optimization_barrier(
+        (grad_out, grad_qkv, grad_up_weight, grad_down_weight)
+    )
+    grad_out_weight, grad_qkv_weight = lax.psum((sent_out, sent_qkv), "dp")
+    partial_one = product_flip(grad_projected, qkv_local).astype(jnp.bfloat16)
+    grad_normed_one = scatter_group(after(partial_one, sent_out, sent_qkv))
+
+    partial_feed = product(activated, down_local).astype(jnp.bfloat16)
+    feed_out = scatter_group(after(partial_feed, grad_normed_one))
+    block_out = (middle + feed_out + bias_down.astype(jnp.float32)).astype(jnp.bfloat16)
 
     centred_one, inverse_one = norm_stats(residual)
     back_one, grad_ln1_gain, grad_ln1_bias = norm_backward(
@@ -303,47 +644,44 @@
     )
     grad_tokens = grad_middle + back_one
 
-    def to_columns(array):
-        return lax.all_to_all(array, "col", split_axis=1, concat_axis=0, tiled=True)
-
-    def dp_sum(array):
-        return lax.psum(array.astype(jnp.bfloat16), "dp").astype(jnp.float32)
-
-    grad_up_weight = dp_sum(lax.all_to_all(grad_up, "col", split_axis=0, concat_axis=1, tiled=True))
-    grad_down_weight = dp_sum(to_columns(grad_down))
-    grad_out_weight = dp_sum(to_columns(grad_out))
     width = local_heads * HD
-    grad_qkv_weight = dp_sum(
-        lax.all_to_all(
-            grad_qkv.reshape(-1, 3, width), "col", split_axis=0, concat_axis=2, tiled=True
-        )
-    )
+    spare = jnp.zeros_like(grad_out_bias)
+    vectors = jnp.stack(
+        [
+            grad_ln1_gain,
+            grad_ln1_bias,
+            grad_out_bias,
+            grad_ln2_gain,
+            grad_ln2_bias,
+            grad_down_bias,
+            spare,
+            spare,
+        ]
+    )
+    block_out, grad_tokens, vectors = exchange(
+        [block_out, grad_tokens.astype(jnp.bfloat16), vectors], (("columns", 1),) * 3, 6
+    )
+    features = tokens.shape[1]
     biases = jnp.concatenate([grad_qv_bias.reshape(-1), grad_up_bias])
-    biases = lax.psum(biases, "dp")
-    vector_sums = lax.psum(
-        jnp.stack(
-            [grad_ln1_gain, grad_ln1_bias, grad_out_bias, grad_ln2_gain, grad_ln2_bias, grad_down_bias]
-        ),
-        ("dp", "row", "col"),
-    )
-    features = tokens.shape[1]
-    vector_sums = lax.dynamic_slice_in_dim(
-        vector_sums, lax.axis_index("col") * features, features, axis=1
-    )
+    biases = jnp.pad(biases, (0, 8 * features - biases.shape[0])).reshape(8, features)
+    vector_sums = total_over_rows(
+        jnp.concatenate([jnp.sum(vectors.reshape(cols, 8, -1), axis=0), biases])
+    )
+    biases = vector_sums[8:].reshape(-1)
     return (
-        to_columns(block_out),
-        to_columns(grad_tokens),
+        block_out,
+        grad_tokens.astype(jnp.float32),
         vector_sums[0],
         vector_sums[1],
-        grad_qkv_weight,
+        grad_qkv_weight.astype(jnp.float32).reshape(qkv_weight.shape),
         biases[: 2 * width].reshape(2, width),
-        grad_out_weight,
+        grad_out_weight.astype(jnp.float32),
         vector_sums[2],
         vector_sums[3],
         vector_sums[4],
-        grad_up_weight,
-        biases[2 * width :],
-        grad_down_weight,
+        grad_up_weight.astype(jnp.float32),
+        biases[2 * width : 2 * width + up_bias.shape[0]],
+        grad_down_weight.astype(jnp.float32),
         vector_sums[5],
     )
 

time: 725 us -> 415 us (0.57)
  waiting for transfers between devices: 366 us -> 0.04 us
  Pallas kernels: 32.1 us -> 310 us
  blocking collectives: 79 us -> 5.22 us
  other arithmetic: 80.6 us -> 21 us
  local copies, waits for them, and re-layouts: 55.8 us -> 20.3 us
  starting transfers between devices: 34.5 us -> 0.08 us
  matrix products: 55.4 us -> 38.2 us
    pallas_call x0 -> x12, Pallas kernels: none -> 269 us  [the longest x4 88.3 us: scatter_group(): pl.pallas_call(scatter_kernel, in_specs=[pl.BlockSpec(memory_space=pltpu....]
    reduce_scatter x4 -> x0, waiting for transfers between devices: 139 us -> none  [scatter_group(): lax.psum_scatter(partial_sum.astype(jnp.bfloat16), GROUP, scatter_dimensi...]
    psum x1 -> x2, waiting for transfers between devices: 88.4 us -> 0.01 us  [the longest x1 0.01 us: on_device(): grad_up_weight, grad_down_weight = lax.psum((grad_up, grad_down), 'dp')]
    all_to_all x9 -> x0, waiting for transfers between devices: 73.2 us -> none  [the longest x1 20.8 us: take_columns(): lax.all_to_all(shard, 'col', split_axis=shard.ndim - 1, concat_axis=0, ti...]
    all_gather x4 -> x0, waiting for transfers between devices: 63.4 us -> none  [the longest x2 59.3 us: gather_group(): return lax.all_gather(shard, GROUP, axis=0, tiled=True)]
    psum x2 -> x0, blocking collectives: 51.8 us -> none  [the longest x1 39.3 us: on_device(): lax.psum(jnp.stack([grad_ln1_gain, grad_ln1_bias, grad_out_bias, grad_ln2...]
    all_to_all x9 -> x0, starting transfers between devices: 34 us -> none  [the longest x4 14.2 us: to_columns(): return lax.all_to_all(array, 'col', split_axis=1, concat_axis=0, tiled=True)]
    reduce_sum x1 -> x2, other arithmetic: 29.7 us -> 1.64 us  [norm_stats(): inverse = lax.rsqrt(jnp.mean(away * away, axis=-1, keepdims=True) + epsilon)]
  transfers between devices with their start and end apart: 18 -> 2, of which waited for: 14 -> 0; matrix products, arithmetic and copies ran while one was open for 13% -> 7% of each run, Pallas kernels for 0% -> 37%
where the time goes in v2:
time: 415 us; the launch traced here: 410 us
  Pallas kernels  310 us (75%)
  matrix products  38.2 us (9%)
  other arithmetic  21 us (5%)
  local copies, waits for them, and re-layouts  20.3 us (5%)
  between operations  15.2 us (4%)
  blocking collectives  5.22 us (1%)
    pallas_call x4, Pallas kernels, scatter_group(): pl.pallas_call(scatter_kernel, in_specs=[pl.BlockSpec(memory_space=pltpu....  88.3 us
    pallas_call x4, Pallas kernels, exchange(): pl.pallas_call(functools.partial(exchange_kernel, plan), in_specs=[pl.Blo...  88 us
    pallas_call x3, Pallas kernels, gather_group(): pl.pallas_call(functools.partial(gather_kernel, tiled, total), in_specs=[...  84.7 us
    pallas_call x1, Pallas kernels, attend_back(): pl.pallas_call(functools.partial(attend_back_kernel, heads, window, scale...  28.2 us
    unnamed x89, local copies, waits for them, and re-layouts  17.8 us
    dot_general x4, matrix products, product_flip(): lax.dot_general(left, right, (((1,), (1,)), ((), ())), preferred_element_...  14.9 us
    pallas_call x1, Pallas kernels, attend(): pl.pallas_call(functools.partial(attend_kernel, heads, window, scale), gr...  12.6 us
    dot_general x4, matrix products, outer_sum(): lax.dot_general(left, right, (((0,), (0,)), ((), ())), preferred_element_...  12.5 us
  transfers between devices with their start and end apart: 2, of which 0 were waited for; matrix products, arithmetic and copies ran while one was open for 7% of the time, Pallas kernels for 37%

profile of v2, /device:TPU:0, one launch (start us, length us, event | category | flops | bytes accessed | tf_op | source)
XLA Modules:
  0.0 409.9 jit_solution(12433489695314001976)
XLA Ops:
  9.3 42.5 %gather_group.3 = (bf16[2048,1024]{1,0:T(8,128)(2,1)S(1)}, bf16[2048,1024]{1,0:T(8,128)(2,1)}) custom-call(bf16[1024,256]{1,0:T(8,128)(2,1)S(1)} %copy-done.11, bf16[1024,256]{1,0:T(8,128)(2,1)S(1)} %copy-done.12), custom_call_target="tpu_custom_call" | custom-call | bytes 67108864 | tf_op jit(solution)/shard_map/gather_group/pallas_call | solution.py:295
  54.1 5.2 %all_gather.3 = bf16[6,1024]{1,0:T(8,128)(2,1)S(1)} all-gather(bf16[6,256]{1,0:T(8,128)(2,1)S(1)} %stack.54), channel_id=1, replica_groups=mesh['dp'=4,'row'=2,'col'=4] {'col'}, dimensions={1}, use_global_device_ids=true | all-gather | bytes 15360 | tf_op jit(solution)/shard_map/all_gather | solution.py:577
  60.7 3.4 fusion.5
  64.1 35.4 %exchange.4 = (bf16[1024,384]{1,0:T(8,128)(2,1)S(1)}, bf16[128,1024]{1,0:T(8,128)(2,1)S(1)}, bf16[1024,512]{1,0:T(8,128)(2,1)S(1)}, bf16[512,1024]{1,0:T(8,128)(2,1)S(1)}) custom-call(bf16[256,1536]{1,0:T(8,128)(2,1)S(1)} %copy.38.refs_0_, bf16[512,256]{1,0:T(8,128)(2,1)S(1)} %copy-done.13, bf16[256,2048]{1,0:T(8,128)(2,1)S(1)} %copy-done.8, ...), custom_call_target="tpu_custom_call" | custom-call | bytes 67108864 | tf_op jit(solution)/shard_map/exchange/pallas_call | solution.py:469
  101.9 12.6 %attend.1 = bf16[2048,128]{1,0:T(8,128)(2,1)S(1)} custom-call(f32[2]{0:T(128)S(1)} %multiply_exponential_fusion.slopes_ref, s32[2048,1]{1,0:T(8,128)S(1)} %copy.39.first_ref, bf16[2048,384]{1,0:T(8,128)(2,1)S(1)} %add_convert_fusion.q_ref.k_ref.v_ref, bf16[2048,384]{1,0:T(8,128)(2,1)S(1)} %add_convert_fusion.q_ref.k_ref.v_ref, ...), custom_call_target="tpu_custom_call" | custom-call | flops 805306368 | bytes 2097152 | tf_op jit(solution)/shard_map/attend/pallas_call | solution.py:144
  115.8 22.6 %scatter_group.4 = f32[256,1024]{1,0:T(8,128)S(1)} custom-call(bf16[2048,1024]{1,0:T(8,128)(2,1)S(1)} %convolution_convert_fusion.3.part_ref), custom_call_target="tpu_custom_call" | custom-call | bytes 67108864 | tf_op jit(solution)/shard_map/scatter_group/pallas_call | solution.py:379
  142.9 21.1 %gather_group.4 = bf16[2048,1024]{1,0:T(8,128)(2,1)S(1)} custom-call(bf16[256,1024]{1,0:T(8,128)(2,1)S(1)} %add_convert_fusion.2.refs_0_), custom_call_target="tpu_custom_call" | custom-call | bytes 67108864 | tf_op jit(solution)/shard_map/gather_group/pallas_call | solution.py:295
  166.5 2.5 convolution_convert_fusion.5.refs_1_
  169.0 4.9 %convert_reduce_fusion.1 = (f32[512]{0:T(512)S(1)}, bf16[2048,512]{1,0:T(8,128)(2,1)S(1)}) fusion(f32[2048,512]{1,0:T(8,128)S(1)} %fusion.31, f32[512]{0:T(512)S(1)} %convert_element_type.116, bf16[2048,1024]{1,0:T(8,128)(2,1)S(1)} %copy-done.30, bf16[512,1024]{1,0:T(8,128)(2,1)S(1)} %copy-done.15), kind=kOutput, calls=%fused_computation.17 | convolution fusion | flops 2171600384 | bytes 11538432 | tf_op jit(solution)/shard_map/dot_general | solution.py:51
  176.3 4.3 %convolution_convert_fusion.1.part_ref = bf16[2048,1024]{1,0:T(8,128)(2,1)} fusion(bf16[2048,512]{1,0:T(8,128)(2,1)S(1)} %get-tuple-element.95, bf16[1024,512]{1,0:T(8,128)(2,1)S(1)} %copy-done.18), kind=kOutput, calls=%fused_computation.20 | convolution fusion | flops 2149580800 | bytes 7340032 | tf_op jit(solution)/shard_map/dot_general | solution.py:51
  180.6 24.1 %exchange.5 = (bf16[256,2048]{1,0:T(8,128)(2,1)S(1)}, bf16[2048,256]{1,0:T(8,128)(2,1)S(1)}) custom-call(bf16[1024,512]{1,0:T(8,128)(2,1)S(1)} %convolution_convert_fusion.6.refs_0_, bf16[512,1024]{1,0:T(8,128)(2,1)S(1)} %convolution_convert_fusion.5.refs_1_), custom_call_target="tpu_custom_call" | custom-call | bytes 67108864 | tf_op jit(solution)/shard_map/exchange/pallas_call | solution.py:469
  208.9 22.3 %scatter_group.5 = f32[256,1024]{1,0:T(8,128)S(1)} custom-call(bf16[2048,1024]{1,0:T(8,128)(2,1)S(1)} %copy-done.6), custom_call_target="tpu_custom_call" | custom-call | bytes 67108864 | tf_op jit(solution)/shard_map/scatter_group/pallas_call | solution.py:379
  234.4 21.1 %gather_group.5 = bf16[2048,1024]{1,0:T(8,128)(2,1)S(1)} custom-call(bf16[256,1024]{1,0:T(8,128)(2,1)S(1)} %convert_element_type.124.refs_0_), custom_call_target="tpu_custom_call" | custom-call | bytes 67108864 | tf_op jit(solution)/shard_map/gather_group/pallas_call | solution.py:295
  258.8 28.2 %attend_back.1 = bf16[2048,384]{1,0:T(8,128)(2,1)S(1)} custom-call(f32[2]{0:T(128)S(1)} %multiply_exponential_fusion.slopes_ref, s32[2048,1]{1,0:T(8,128)S(1)} %copy.39.first_ref, bf16[2048,384]{1,0:T(8,128)(2,1)S(1)} %add_convert_fusion.q_ref.k_ref.v_ref, bf16[2048,384]{1,0:T(8,128)(2,1)S(1)} %add_convert_fusion.q_ref.k_ref.v_ref, ...), custom_call_target="tpu_custom_call" | custom-call | flops 2013265920 | bytes 3670016 | tf_op jit(solution)/shard_map/attend_back/pallas_call | solution.py:165
  288.5 3.0 convolution_convert_fusion.8.refs_0_
  291.5 4.6 %convolution_convert_fusion.7.refs_1_ = bf16[1024,384]{1,0:T(8,128)(2,1)S(1)} fusion(bf16[2048,1024]{1,0:T(8,128)(2,1)} %copy-done.26, bf16[2048,384]{1,0:T(8,128)(2,1)S(1)} %copy-done.3), kind=kOutput, calls=%fused_computation.31 | convolution fusion | flops 1611005952 | bytes 6553600 | tf_op jit(solution)/shard_map/dot_general | solution.py:55
  296.1 13.7 %exchange.6 = (bf16[512,256]{1,0:T(8,128)(2,1)}, bf16[256,1536]{1,0:T(8,128)(2,1)S(1)}) custom-call(bf16[128,1024]{1,0:T(8,128)(2,1)S(1)} %convolution_convert_fusion.8.refs_0_, bf16[1024,384]{1,0:T(8,128)(2,1)S(1)} %convolution_convert_fusion.7.refs_1_), custom_call_target="tpu_custom_call" | custom-call | bytes 67108864 | tf_op jit(solution)/shard_map/exchange/pallas_call | solution.py:469
  309.9 4.4 %convolution_convert_fusion.part_ref = bf16[2048,1024]{1,0:T(8,128)(2,1)} fusion(bf16[2048,384]{1,0:T(8,128)(2,1)S(1)} %copy-done.3, bf16[1024,384]{1,0:T(8,128)(2,1)S(1)} %copy-done.20), kind=kOutput, calls=%fused_computation.19 | convolution fusion | flops 1612709888 | bytes 6553600 | tf_op jit(solution)/shard_map/dot_general | solution.py:51
  314.2 4.9 %convolution_convert_fusion.2.part_ref = bf16[2048,1024]{1,0:T(8,128)(2,1)} fusion(bf16[512,1024]{1,0:T(8,128)(2,1)S(1)} %copy-done.16, f32[2048,512]{1,0:T(8,128)S(1)} %copy-done.41, f32[512]{0:T(512)S(1)} %convert_element_type.116), kind=kOutput, calls=%fused_computation.21 | convolution fusion | flops 2160066560 | bytes 9439232 | tf_op jit(solution)/shard_map/dot_general | solution.py:47
  322.5 22.0 %scatter_group.6 = f32[256,1024]{1,0:T(8,128)S(1)} custom-call(bf16[2048,1024]{1,0:T(8,128)(2,1)S(1)} %copy-done.5), custom_call_target="tpu_custom_call" | custom-call | bytes 67108864 | tf_op jit(solution)/shard_map/scatter_group/pallas_call | solution.py:379
  346.3 21.4 %scatter_group.7 = f32[256,1024]{1,0:T(8,128)S(1)} custom-call(bf16[2048,1024]{1,0:T(8,128)(2,1)S(1)} %copy-done.4), custom_call_target="tpu_custom_call" | custom-call | bytes 67108864 | tf_op jit(solution)/shard_map/scatter_group/pallas_call | solution.py:379
  369.6 14.9 %exchange.7 = (bf16[1024,256]{1,0:T(8,128)(2,1)S(1)}, bf16[1024,256]{1,0:T(8,128)(2,1)S(1)}, f32[32,256]{1,0:T(8,128)S(1)}) custom-call(bf16[256,1024]{1,0:T(8,128)(2,1)S(1)} %add_convert_fusion.1.refs_0_, bf16[256,1024]{1,0:T(8,128)(2,1)S(1)} %fusion.22.refs_1_, f32[8,1024]{1,0:T(8,128)S(1)} %stack.62.refs_2_), custom_call_target="tpu_custom_call" | custom-call | bytes 67108864 | tf_op jit(solution)/shard_map/exchange/pallas_call | solution.py:469
  384.5 7.9 %total_over_rows.1 = f32[16,256]{1,0:T(8,128)S(1)} custom-call(f32[16,256]{1,0:T(8,128)S(1)} %pad_maximum_fusion.block_ref), custom_call_target="tpu_custom_call" | custom-call | tf_op jit(solution)/shard_map/total_over_rows/pallas_call | solution.py:517
  397.7 2.6 copy.42
  (153 shorter events, 45.1 us)
Async XLA Ops:
  7.2 311.9 %all-reduce.8.cloned.1.call-start = ((), (), s32[]{:S(2)}) async-start(), calls=%async_computation.1 | async-start | bytes 4194304 | tf_op jit(solution)/shard_map/psum | solution.py:612
  51.9 7.5 %copy-start.29 = (bf16[256,3,512]{2,0,1:T(8,128)(2,1)S(1)}, bf16[256,3,512]{2,0,1:T(8,128)(2,1)}, u32[]{:S(2)}) copy-start(bf16[256,3,512]{2,0,1:T(8,128)(2,1)} %param.19) | copy-start | bytes 2359300
  52.5 7.4 %copy-start.31 = (bf16[2,128]{1,0:T(2,128)(2,1)S(1)}, bf16[2,128]{1,0:T(2,128)(2,1)}, u32[]{:S(2)}) copy-start(bf16[2,128]{1,0:T(2,128)(2,1)} %param.20) | copy-start | bytes 1540
  52.5 7.5 %copy-start.39 = (s32[1,9]{1,0:T(1,128)S(1)}, s32[1,9]{1,0:T(1,128)}, u32[]{:S(2)}) copy-start(s32[1,9]{1,0:T(1,128)} %param.16) | copy-start | bytes 112
  60.7 3.5 copy-start.8
  60.7 3.4 copy-start.13
  64.1 37.8 %copy-start.26 = (bf16[2048,1024]{1,0:T(8,128)(2,1)}, bf16[2048,1024]{1,0:T(8,128)(2,1)S(1)}, u32[]{:S(2)}) copy-start(bf16[2048,1024]{1,0:T(8,128)(2,1)S(1)} %fusion.5) | copy-start | bytes 12582916
  99.5 2.4 copy-start.14
  142.3 24.1 %copy-start.21 = (f32[256,1024]{1,0:T(8,128)}, f32[256,1024]{1,0:T(8,128)S(1)}, u32[]{:S(2)}) copy-start(f32[256,1024]{1,0:T(8,128)S(1)} %get-tuple-element.99) | copy-start | bytes 3145732
  142.3 21.7 %copy-start.32 = (bf16[512]{0:T(512)(128)(2,1)S(1)}, bf16[512]{0:T(512)(128)(2,1)}, u32[]{:S(2)}) copy-start(bf16[512]{0:T(512)(128)(2,1)} %param.26) | copy-start | bytes 3076
  142.4 21.7 %copy-start.18 = (bf16[1024,512]{1,0:T(8,128)(2,1)S(1)}, bf16[1024,512]{1,0:T(8,128)(2,1)}, u32[]{:S(2)}) copy-start(bf16[1024,512]{1,0:T(8,128)(2,1)} %copy-done.17) | copy-start | bytes 3145732
  166.4 2.5 copy-start.40
  166.5 2.5 copy-start.15
  206.7 191.0 %all-reduce.6.cloned.1.call-start = ((), (), s32[]{:S(2)}) async-start(), calls=%async_computation | async-start | bytes 2097152 | tf_op jit(solution)/shard_map/psum | solution.py:633
  208.9 22.3 %copy-start.22 = (f32[256,1024]{1,0:T(8,128)S(1)}, f32[256,1024]{1,0:T(8,128)}, u32[]{:S(2)}) copy-start(f32[256,1024]{1,0:T(8,128)} %copy-done.21) | copy-start | bytes 3145732
  288.4 3.1 copy-start.3
  291.5 18.3 %copy-start.20 = (bf16[1024,384]{1,0:T(8,128)(2,1)S(1)}, bf16[1024,384]{1,0:T(8,128)(2,1)}, u32[]{:S(2)}) copy-start(bf16[1024,384]{1,0:T(8,128)(2,1)} %copy-done.19) | copy-start | bytes 2359300
  309.8 4.4 %copy-start.16 = (bf16[512,1024]{1,0:T(8,128)(2,1)S(1)}, bf16[512,1024]{1,0:T(8,128)(2,1)}, u32[]{:S(2)}) copy-start(bf16[512,1024]{1,0:T(8,128)(2,1)} %copy-done.14) | copy-start | bytes 3145732
  309.9 4.4 %copy-start.41 = (f32[2048,512]{1,0:T(8,128)S(1)}, f32[2048,512]{1,0:T(8,128)}, u32[]{:S(2)}) copy-start(f32[2048,512]{1,0:T(8,128)} %copy-done.40) | copy-start | bytes 12582916
  322.5 23.8 %copy-start.4 = (bf16[2048,1024]{1,0:T(8,128)(2,1)S(1)}, bf16[2048,1024]{1,0:T(8,128)(2,1)}, u32[]{:S(2)}) copy-start(bf16[2048,1024]{1,0:T(8,128)(2,1)} %convolution_convert_fusion.2.part_ref) | copy-start | bytes 12582916
  344.5 23.1 %copy-start.23 = (f32[256,1024]{1,0:T(8,128)S(1)}, f32[256,1024]{1,0:T(8,128)}, u32[]{:S(2)}) copy-start(f32[256,1024]{1,0:T(8,128)} %copy-done.21) | copy-start | bytes 3145732
  346.2 21.7 %copy-start.25 = (f32[256,1024]{1,0:T(8,128)S(1)}, f32[256,1024]{1,0:T(8,128)}, u32[]{:S(2)}) copy-start(f32[256,1024]{1,0:T(8,128)} %copy-done.24) | copy-start | bytes 3145732
  368.0 26.1 %copy-start.28 = (bf16[256,2048]{1,0:T(8,128)(2,1)S(1)}, bf16[256,2048]{1,0:T(8,128)(2,1)}, u32[]{:S(2)}) copy-start(bf16[256,2048]{1,0:T(8,128)(2,1)} %get-tuple-element.52) | copy-start | bytes 3145732
  368.0 27.7 %copy-start.27 = (bf16[2048,256]{1,0:T(8,128)(2,1)S(1)}, bf16[2048,256]{1,0:T(8,128)(2,1)}, u32[]{:S(2)}) copy-start(bf16[2048,256]{1,0:T(8,128)(2,1)} %get-tuple-element.53) | copy-start | bytes 3145732
  (20 other events, 35.9 us)
Sparse Core Ops, SparseCore 0:
  206.8 88.3 all-reduce.7
  320.4 52.7 all-reduce.5

commit v3 on v2

--- a/solution.py
+++ b/solution.py
@@ -11,7 +11,7 @@
 HD = 64
 HEADS = 16
 LONGEST = 512
-BLOCK = 256
+BLOCK = 128
 
 epsilon = 1e-05
 masked = -1e30

time: 415 us -> 429 us (1.034)
  Pallas kernels: 310 us -> 325 us
    pallas_call x1, Pallas kernels: 28.2 us -> 36.8 us  [attend_back(): pl.pallas_call(functools.partial(attend_back_kernel, heads, window, scale...]
    pallas_call x1, Pallas kernels: 12.6 us -> 18.9 us  [attend(): pl.pallas_call(functools.partial(attend_kernel, heads, window, scale), gr...]
  transfers between devices with their start and end apart: 2 -> 2, of which waited for: 0 -> 0; matrix products, arithmetic and copies ran while one was open for 7% -> 7% of each run, Pallas kernels for 37% -> 38%
where the time goes in v3:
time: 429 us; the launch traced here: 425 us
  Pallas kernels  325 us (76%)
  matrix products  38.2 us (9%)
  other arithmetic  21 us (5%)
  local copies, waits for them, and re-layouts  20.3 us (5%)
  between operations  15.2 us (4%)
  blocking collectives  5.22 us (1%)
    pallas_call x4, Pallas kernels, scatter_group(): pl.pallas_call(scatter_kernel, in_specs=[pl.BlockSpec(memory_space=pltpu....  88.4 us
    pallas_call x4, Pallas kernels, exchange(): pl.pallas_call(functools.partial(exchange_kernel, plan), in_specs=[pl.Blo...  88 us
    pallas_call x3, Pallas kernels, gather_group(): pl.pallas_call(functools.partial(gather_kernel, tiled, total), in_specs=[...  84.7 us
    pallas_call x1, Pallas kernels, attend_back(): pl.pallas_call(functools.partial(attend_back_kernel, heads, window, scale...  36.8 us
    pallas_call x1, Pallas kernels, attend(): pl.pallas_call(functools.partial(attend_kernel, heads, window, scale), gr...  18.9 us
    unnamed x89, local copies, waits for them, and re-layouts  17.8 us
    dot_general x4, matrix products, product_flip(): lax.dot_general(left, right, (((1,), (1,)), ((), ())), preferred_element_...  14.9 us
    dot_general x4, matrix products, outer_sum(): lax.dot_general(left, right, (((0,), (0,)), ((), ())), preferred_element_...  12.5 us
  transfers between devices with their start and end apart: 2, of which 0 were waited for; matrix products, arithmetic and copies ran while one was open for 7% of the time, Pallas kernels for 38%

profile of v3, /device:TPU:0, one launch (start us, length us, event | category | flops | bytes accessed | tf_op | source)
XLA Modules:
  0.0 424.7 jit_solution(3302721903074905264)
XLA Ops:
  9.3 42.5 %gather_group.3 = (bf16[2048,1024]{1,0:T(8,128)(2,1)S(1)}, bf16[2048,1024]{1,0:T(8,128)(2,1)}) custom-call(bf16[1024,256]{1,0:T(8,128)(2,1)S(1)} %copy-done.11, bf16[1024,256]{1,0:T(8,128)(2,1)S(1)} %copy-done.12), custom_call_target="tpu_custom_call" | custom-call | bytes 67108864 | tf_op jit(solution)/shard_map/gather_group/pallas_call | solution.py:295
  54.1 5.2 %all_gather.3 = bf16[6,1024]{1,0:T(8,128)(2,1)S(1)} all-gather(bf16[6,256]{1,0:T(8,128)(2,1)S(1)} %stack.54), channel_id=1, replica_groups=mesh['dp'=4,'row'=2,'col'=4] {'col'}, dimensions={1}, use_global_device_ids=true | all-gather | bytes 15360 | tf_op jit(solution)/shard_map/all_gather | solution.py:577
  60.7 3.4 fusion.5
  64.1 35.4 %exchange.4 = (bf16[1024,384]{1,0:T(8,128)(2,1)S(1)}, bf16[128,1024]{1,0:T(8,128)(2,1)S(1)}, bf16[1024,512]{1,0:T(8,128)(2,1)S(1)}, bf16[512,1024]{1,0:T(8,128)(2,1)S(1)}) custom-call(bf16[256,1536]{1,0:T(8,128)(2,1)S(1)} %copy.38.refs_0_, bf16[512,256]{1,0:T(8,128)(2,1)S(1)} %copy-done.13, bf16[256,2048]{1,0:T(8,128)(2,1)S(1)} %copy-done.8, ...), custom_call_target="tpu_custom_call" | custom-call | bytes 67108864 | tf_op jit(solution)/shard_map/exchange/pallas_call | solution.py:469
  101.9 18.9 %attend.1 = bf16[2048,128]{1,0:T(8,128)(2,1)S(1)} custom-call(f32[2]{0:T(128)S(1)} %multiply_exponential_fusion.slopes_ref, s32[2048,1]{1,0:T(8,128)S(1)} %copy.39.first_ref, bf16[2048,384]{1,0:T(8,128)(2,1)S(1)} %add_convert_fusion.q_ref.k_ref.v_ref, bf16[2048,384]{1,0:T(8,128)(2,1)S(1)} %add_convert_fusion.q_ref.k_ref.v_ref, ...), custom_call_target="tpu_custom_call" | custom-call | flops 671088640 | bytes 2097152 | tf_op jit(solution)/shard_map/attend/pallas_call | solution.py:144
  122.1 22.6 %scatter_group.4 = f32[256,1024]{1,0:T(8,128)S(1)} custom-call(bf16[2048,1024]{1,0:T(8,128)(2,1)S(1)} %convolution_convert_fusion.3.part_ref), custom_call_target="tpu_custom_call" | custom-call | bytes 67108864 | tf_op jit(solution)/shard_map/scatter_group/pallas_call | solution.py:379
  149.2 21.1 %gather_group.4 = bf16[2048,1024]{1,0:T(8,128)(2,1)S(1)} custom-call(bf16[256,1024]{1,0:T(8,128)(2,1)S(1)} %add_convert_fusion.2.refs_0_), custom_call_target="tpu_custom_call" | custom-call | bytes 67108864 | tf_op jit(solution)/shard_map/gather_group/pallas_call | solution.py:295
  172.7 2.5 convolution_convert_fusion.5.refs_1_
  175.2 4.9 %convert_reduce_fusion.1 = (f32[512]{0:T(512)S(1)}, bf16[2048,512]{1,0:T(8,128)(2,1)S(1)}) fusion(f32[2048,512]{1,0:T(8,128)S(1)} %fusion.31, f32[512]{0:T(512)S(1)} %convert_element_type.116, bf16[2048,1024]{1,0:T(8,128)(2,1)S(1)} %copy-done.30, bf16[512,1024]{1,0:T(8,128)(2,1)S(1)} %copy-done.15), kind=kOutput, calls=%fused_computation.17 | convolution fusion | flops 2171600384 | bytes 11538432 | tf_op jit(solution)/shard_map/dot_general | solution.py:51
  182.6 4.3 %convolution_convert_fusion.1.part_ref = bf16[2048,1024]{1,0:T(8,128)(2,1)} fusion(bf16[2048,512]{1,0:T(8,128)(2,1)S(1)} %get-tuple-element.95, bf16[1024,512]{1,0:T(8,128)(2,1)S(1)} %copy-done.18), kind=kOutput, calls=%fused_computation.20 | convolution fusion | flops 2149580800 | bytes 7340032 | tf_op jit(solution)/shard_map/dot_general | solution.py:51
  186.9 24.1 %exchange.5 = (bf16[256,2048]{1,0:T(8,128)(2,1)S(1)}, bf16[2048,256]{1,0:T(8,128)(2,1)S(1)}) custom-call(bf16[1024,512]{1,0:T(8,128)(2,1)S(1)} %convolution_convert_fusion.6.refs_0_, bf16[512,1024]{1,0:T(8,128)(2,1)S(1)} %convolution_convert_fusion.5.refs_1_), custom_call_target="tpu_custom_call" | custom-call | bytes 67108864 | tf_op jit(solution)/shard_map/exchange/pallas_call | solution.py:469
  215.2 22.3 %scatter_group.5 = f32[256,1024]{1,0:T(8,128)S(1)} custom-call(bf16[2048,1024]{1,0:T(8,128)(2,1)S(1)} %copy-done.6), custom_call_target="tpu_custom_call" | custom-call | bytes 67108864 | tf_op jit(solution)/shard_map/scatter_group/pallas_call | solution.py:379
  240.7 21.1 %gather_group.5 = bf16[2048,1024]{1,0:T(8,128)(2,1)S(1)} custom-call(bf16[256,1024]{1,0:T(8,128)(2,1)S(1)} %convert_element_type.124.refs_0_), custom_call_target="tpu_custom_call" | custom-call | bytes 67108864 | tf_op jit(solution)/shard_map/gather_group/pallas_call | solution.py:295
  265.0 36.8 %attend_back.1 = bf16[2048,384]{1,0:T(8,128)(2,1)S(1)} custom-call(f32[2]{0:T(128)S(1)} %multiply_exponential_fusion.slopes_ref, s32[2048,1]{1,0:T(8,128)S(1)} %copy.39.first_ref, bf16[2048,384]{1,0:T(8,128)(2,1)S(1)} %add_convert_fusion.q_ref.k_ref.v_ref, bf16[2048,384]{1,0:T(8,128)(2,1)S(1)} %add_convert_fusion.q_ref.k_ref.v_ref, ...), custom_call_target="tpu_custom_call" | custom-call | flops 1677721600 | bytes 3670016 | tf_op jit(solution)/shard_map/attend_back/pallas_call | solution.py:165
  303.3 3.0 convolution_convert_fusion.8.refs_0_
  306.4 4.6 %convolution_convert_fusion.7.refs_1_ = bf16[1024,384]{1,0:T(8,128)(2,1)S(1)} fusion(bf16[2048,1024]{1,0:T(8,128)(2,1)} %copy-done.26, bf16[2048,384]{1,0:T(8,128)(2,1)S(1)} %copy-done.3), kind=kOutput, calls=%fused_computation.31 | convolution fusion | flops 1611005952 | bytes 6553600 | tf_op jit(solution)/shard_map/dot_general | solution.py:55
  311.0 13.7 %exchange.6 = (bf16[512,256]{1,0:T(8,128)(2,1)}, bf16[256,1536]{1,0:T(8,128)(2,1)S(1)}) custom-call(bf16[128,1024]{1,0:T(8,128)(2,1)S(1)} %convolution_convert_fusion.8.refs_0_, bf16[1024,384]{1,0:T(8,128)(2,1)S(1)} %convolution_convert_fusion.7.refs_1_), custom_call_target="tpu_custom_call" | custom-call | bytes 67108864 | tf_op jit(solution)/shard_map/exchange/pallas_call | solution.py:469
  324.7 4.4 %convolution_convert_fusion.part_ref = bf16[2048,1024]{1,0:T(8,128)(2,1)} fusion(bf16[2048,384]{1,0:T(8,128)(2,1)S(1)} %copy-done.3, bf16[1024,384]{1,0:T(8,128)(2,1)S(1)} %copy-done.20), kind=kOutput, calls=%fused_computation.19 | convolution fusion | flops 1612709888 | bytes 6553600 | tf_op jit(solution)/shard_map/dot_general | solution.py:51
  329.1 4.9 %convolution_convert_fusion.2.part_ref = bf16[2048,1024]{1,0:T(8,128)(2,1)} fusion(bf16[512,1024]{1,0:T(8,128)(2,1)S(1)} %copy-done.16, f32[2048,512]{1,0:T(8,128)S(1)} %copy-done.41, f32[512]{0:T(512)S(1)} %convert_element_type.116), kind=kOutput, calls=%fused_computation.21 | convolution fusion | flops 2160066560 | bytes 9439232 | tf_op jit(solution)/shard_map/dot_general | solution.py:47
  337.4 22.0 %scatter_group.6 = f32[256,1024]{1,0:T(8,128)S(1)} custom-call(bf16[2048,1024]{1,0:T(8,128)(2,1)S(1)} %copy-done.5), custom_call_target="tpu_custom_call" | custom-call | bytes 67108864 | tf_op jit(solution)/shard_map/scatter_group/pallas_call | solution.py:379
  361.1 21.4 %scatter_group.7 = f32[256,1024]{1,0:T(8,128)S(1)} custom-call(bf16[2048,1024]{1,0:T(8,128)(2,1)S(1)} %copy-done.4), custom_call_target="tpu_custom_call" | custom-call | bytes 67108864 | tf_op jit(solution)/shard_map/scatter_group/pallas_call | solution.py:379
  384.5 14.9 %exchange.7 = (bf16[1024,256]{1,0:T(8,128)(2,1)S(1)}, bf16[1024,256]{1,0:T(8,128)(2,1)S(1)}, f32[32,256]{1,0:T(8,128)S(1)}) custom-call(bf16[256,1024]{1,0:T(8,128)(2,1)S(1)} %add_convert_fusion.1.refs_0_, bf16[256,1024]{1,0:T(8,128)(2,1)S(1)} %fusion.22.refs_1_, f32[8,1024]{1,0:T(8,128)S(1)} %stack.62.refs_2_), custom_call_target="tpu_custom_call" | custom-call | bytes 67108864 | tf_op jit(solution)/shard_map/exchange/pallas_call | solution.py:469
  399.4 7.9 %total_over_rows.1 = f32[16,256]{1,0:T(8,128)S(1)} custom-call(f32[16,256]{1,0:T(8,128)S(1)} %pad_maximum_fusion.block_ref), custom_call_target="tpu_custom_call" | custom-call | tf_op jit(solution)/shard_map/total_over_rows/pallas_call | solution.py:517
  412.6 2.6 copy.42
  (153 shorter events, 45.0 us)
Async XLA Ops:
  7.2 326.8 %all-reduce.8.cloned.1.call-start = ((), (), s32[]{:S(2)}) async-start(), calls=%async_computation.1 | async-start | bytes 4194304 | tf_op jit(solution)/shard_map/psum | solution.py:612
  51.9 7.5 %copy-start.29 = (bf16[256,3,512]{2,0,1:T(8,128)(2,1)S(1)}, bf16[256,3,512]{2,0,1:T(8,128)(2,1)}, u32[]{:S(2)}) copy-start(bf16[256,3,512]{2,0,1:T(8,128)(2,1)} %param.19) | copy-start | bytes 2359300
  52.5 7.4 %copy-start.31 = (bf16[2,128]{1,0:T(2,128)(2,1)S(1)}, bf16[2,128]{1,0:T(2,128)(2,1)}, u32[]{:S(2)}) copy-start(bf16[2,128]{1,0:T(2,128)(2,1)} %param.20) | copy-start | bytes 1540
  52.5 7.5 %copy-start.39 = (s32[1,9]{1,0:T(1,128)S(1)}, s32[1,9]{1,0:T(1,128)}, u32[]{:S(2)}) copy-start(s32[1,9]{1,0:T(1,128)} %param.16) | copy-start | bytes 112
  60.7 3.5 copy-start.8
  60.7 3.4 copy-start.13
  64.1 37.8 %copy-start.26 = (bf16[2048,1024]{1,0:T(8,128)(2,1)}, bf16[2048,1024]{1,0:T(8,128)(2,1)S(1)}, u32[]{:S(2)}) copy-start(bf16[2048,1024]{1,0:T(8,128)(2,1)S(1)} %fusion.5) | copy-start | bytes 12582916
  99.5 2.4 copy-start.14
  148.6 24.1 %copy-start.21 = (f32[256,1024]{1,0:T(8,128)}, f32[256,1024]{1,0:T(8,128)S(1)}, u32[]{:S(2)}) copy-start(f32[256,1024]{1,0:T(8,128)S(1)} %get-tuple-element.99) | copy-start | bytes 3145732
  148.6 21.7 %copy-start.32 = (bf16[512]{0:T(512)(128)(2,1)S(1)}, bf16[512]{0:T(512)(128)(2,1)}, u32[]{:S(2)}) copy-start(bf16[512]{0:T(512)(128)(2,1)} %param.26) | copy-start | bytes 3076
  148.6 21.7 %copy-start.18 = (bf16[1024,512]{1,0:T(8,128)(2,1)S(1)}, bf16[1024,512]{1,0:T(8,128)(2,1)}, u32[]{:S(2)}) copy-start(bf16[1024,512]{1,0:T(8,128)(2,1)} %copy-done.17) | copy-start | bytes 3145732
  172.7 2.5 copy-start.40
  172.7 2.5 copy-start.15
  213.0 199.6 %all-reduce.6.cloned.1.call-start = ((), (), s32[]{:S(2)}) async-start(), calls=%async_computation | async-start | bytes 2097152 | tf_op jit(solution)/shard_map/psum | solution.py:633
  215.2 22.3 %copy-start.22 = (f32[256,1024]{1,0:T(8,128)S(1)}, f32[256,1024]{1,0:T(8,128)}, u32[]{:S(2)}) copy-start(f32[256,1024]{1,0:T(8,128)} %copy-done.21) | copy-start | bytes 3145732
  303.3 3.1 copy-start.3
  306.4 18.3 %copy-start.20 = (bf16[1024,384]{1,0:T(8,128)(2,1)S(1)}, bf16[1024,384]{1,0:T(8,128)(2,1)}, u32[]{:S(2)}) copy-start(bf16[1024,384]{1,0:T(8,128)(2,1)} %copy-done.19) | copy-start | bytes 2359300
  324.7 4.4 %copy-start.16 = (bf16[512,1024]{1,0:T(8,128)(2,1)S(1)}, bf16[512,1024]{1,0:T(8,128)(2,1)}, u32[]{:S(2)}) copy-start(bf16[512,1024]{1,0:T(8,128)(2,1)} %copy-done.14) | copy-start | bytes 3145732
  324.7 4.4 %copy-start.41 = (f32[2048,512]{1,0:T(8,128)S(1)}, f32[2048,512]{1,0:T(8,128)}, u32[]{:S(2)}) copy-start(f32[2048,512]{1,0:T(8,128)} %copy-done.40) | copy-start | bytes 12582916
  337.4 23.8 %copy-start.4 = (bf16[2048,1024]{1,0:T(8,128)(2,1)S(1)}, bf16[2048,1024]{1,0:T(8,128)(2,1)}, u32[]{:S(2)}) copy-start(bf16[2048,1024]{1,0:T(8,128)(2,1)} %convolution_convert_fusion.2.part_ref) | copy-start | bytes 12582916
  359.4 23.1 %copy-start.23 = (f32[256,1024]{1,0:T(8,128)S(1)}, f32[256,1024]{1,0:T(8,128)}, u32[]{:S(2)}) copy-start(f32[256,1024]{1,0:T(8,128)} %copy-done.21) | copy-start | bytes 3145732
  361.1 21.7 %copy-start.25 = (f32[256,1024]{1,0:T(8,128)S(1)}, f32[256,1024]{1,0:T(8,128)}, u32[]{:S(2)}) copy-start(f32[256,1024]{1,0:T(8,128)} %copy-done.24) | copy-start | bytes 3145732
  382.8 26.1 %copy-start.28 = (bf16[256,2048]{1,0:T(8,128)(2,1)S(1)}, bf16[256,2048]{1,0:T(8,128)(2,1)}, u32[]{:S(2)}) copy-start(bf16[256,2048]{1,0:T(8,128)(2,1)} %get-tuple-element.52) | copy-start | bytes 3145732
  382.9 27.6 %copy-start.27 = (bf16[2048,256]{1,0:T(8,128)(2,1)S(1)}, bf16[2048,256]{1,0:T(8,128)(2,1)}, u32[]{:S(2)}) copy-start(bf16[2048,256]{1,0:T(8,128)(2,1)} %get-tuple-element.53) | copy-start | bytes 3145732
  (20 other events, 35.9 us)
Sparse Core Ops, SparseCore 0:
  213.1 88.3 all-reduce.7
  335.3 52.8 all-reduce.5
